TPU v7x, 512 devices: a whole 4x4x16 slice. The times are simulated.
512 devices in a mesh: row: 16 (over z_lo, y), col: 32 (over x, z_hi, core).
Axes of the slice: x: 4, y: 4, z: 16 (z_hi: 4, z_lo: 4; z = z_hi * 4 + z_lo), core: 2. Of those that a mesh axis runs over, the one named last changes fastest.
Arguments:
- points: float32 [16, 65536], P(None, ('row', 'col')), may hold values from 0 to 1
- lengthscales: float32 [16], replicated, may hold values from 0.25 to 0.5
- variances: float32 [2], replicated, may hold values from 0.5 to 2
- factor: float32 [128, 65536], P(None, ('row', 'col')), may hold values from -0.5 to 0.5
- solution: float32 [16, 65536], P(None, ('row', 'col')), may hold values from -6 to 6
- residual: float32 [16, 65536], P(None, ('row', 'col')), may hold values from -48 to 48
- direction: float32 [16, 65536], P(None, ('row', 'col')), may hold values from -48 to 48
Outputs:
- new_solution: float32 [16, 65536], P(None, ('row', 'col'))
- new_residual: float32 [16, 65536], P(None, ('row', 'col'))
- new_direction: float32 [16, 65536], P(None, ('row', 'col'))
All inputs are finite; a program needn't handle non-finite values.
Results may differ from a plain program's by a relative error of at most 0.0003.
Values sent between devices are 32-bit elements; how exact they have to be, the bound alone decides.
A program may use at most 64 MiB of HBM per device.

v0:
```python
import jax
import jax.numpy as jnp
from jax import lax
from jax.sharding import PartitionSpec as P

root_five = 5.0**0.5
highest = lax.Precision.HIGHEST


def matern(cross, sq_left, sq_right, signal):
    dist_sq = jnp.maximum(sq_left[:, None] + sq_right[None, :] - 2.0 * cross, 0.0)
    dist = jnp.sqrt(dist_sq)
    return signal * (1.0 + root_five * dist + 5.0 / 3.0 * dist_sq) * jnp.exp(-root_five * dist)


def pair_terms(
    left_pts, left_sq, left_dir, right_pts, right_sq, right_dir, left_weight, right_weight, signal
):
    rows = left_pts.shape[1]
    piece = min(512, rows)
    left_out = []
    right_out = jnp.zeros((right_dir.shape[0], right_pts.shape[1]), jnp.float32)
    for start in range(0, rows, piece):
        block_pts = left_pts[:, start : start + piece]
        cross = lax.dot_general(block_pts, right_pts, (((0,), (0,)), ((), ())), precision=highest)
        kernel = matern(cross, left_sq[start : start + piece], right_sq, signal)
        to_left = lax.dot_general(right_dir, kernel, (((1,), (1,)), ((), ())), precision=highest)
        left_out.append(to_left * left_weight[None, start : start + piece])
        weighted = left_dir[:, start : start + piece] * right_weight[None, start : start + piece]
        right_out = right_out + jnp.dot(weighted, kernel, precision=highest)
    return (jnp.concatenate(left_out, axis=1), right_out)


def local(points, lengthscales, variances, factor, solution, residual, direction):
    signal = variances[0]
    noise = variances[1]
    own = points.shape[1]
    probes = direction.shape[0]
    row_count = lax.axis_size("row")
    col_count = lax.axis_size("col")
    my_row = lax.axis_index("row")
    my_col = lax.axis_index("col")
    scaled = points / lengthscales[:, None]
    col_pts, col_dir = (
        lax.all_gather(scaled, "row", axis=1, tiled=True),
        lax.all_gather(direction, "row", axis=1, tiled=True),
    )
    col_sq = jnp.sum(col_pts * col_pts, axis=0)
    eye_rank = jnp.eye(factor.shape[0], dtype=jnp.float32)
    gram_local = jnp.dot(factor, factor.T, precision=highest)
    proj_local = jnp.dot(residual, factor.T, precision=highest)
    gram, proj_res = lax.psum((gram_local, proj_local), ("row", "col"))
    chol = jnp.linalg.cholesky(gram + noise * eye_rank)
    coef = jax.scipy.linalg.cho_solve((chol, True), proj_res.T)
    precond_res = (residual - jnp.dot(coef.T, factor, precision=highest)) / noise
    first_local = jnp.sum(residual * precond_res, axis=1)

    def column_slices(block):
        right_pts = lax.dynamic_slice_in_dim(col_pts, block * own, own, 1)
        right_sq = lax.dynamic_slice_in_dim(col_sq, block * own, own, 0)
        right_dir = lax.dynamic_slice_in_dim(col_dir, block * own, own, 1)
        return (right_pts, right_sq, right_dir)

    row_pts, row_dir = (
        lax.all_gather(scaled, "col", axis=1, tiled=True),
        lax.all_gather(direction, "col", axis=1, tiled=True),
    )
    row_sq = jnp.sum(row_pts * row_pts, axis=0)
    sub_index = jnp.arange(col_count, dtype=jnp.int32)

    def upper_step(acc, block):
        right_pts, right_sq, right_dir = column_slices(block)
        later = block > my_row
        left_weight = jnp.repeat(
            jnp.where(later, True, sub_index <= my_col).astype(jnp.float32), own
        )
        right_weight = jnp.repeat(
            jnp.where(later, True, sub_index < my_col).astype(jnp.float32), own
        )

        def active(unused):
            return pair_terms(
                row_pts,
                row_sq,
                row_dir,
                right_pts,
                right_sq,
                right_dir,
                left_weight,
                right_weight,
                signal,
            )

        def skipped(unused):
            return (
                jnp.zeros((probes, row_pts.shape[1]), jnp.float32),
                jnp.zeros((probes, own), jnp.float32),
            )

        left_part, right_part = lax.cond(block >= my_row, active, skipped, 0)
        return (acc + left_part, right_part)

    start = jnp.zeros((probes, row_pts.shape[1]), jnp.float32)
    acc, right_parts = lax.scan(upper_step, start, jnp.arange(row_count, dtype=jnp.int32))
    row_sum = lax.psum_scatter(acc, "col", scatter_dimension=1, tiled=True)
    col_sum = lax.psum_scatter(right_parts, "row", scatter_dimension=0, tiled=True)
    image = row_sum + col_sum[0] + noise * direction
    res_z, curvature = lax.psum((first_local, jnp.sum(direction * image, axis=1)), ("row", "col"))
    alpha = res_z / curvature
    new_solution = solution + alpha[:, None] * direction
    new_residual = residual - alpha[:, None] * image
    proj_new = lax.psum(jnp.dot(new_residual, factor.T, precision=highest), ("row", "col"))
    coef_new = jax.scipy.linalg.cho_solve((chol, True), proj_new.T)
    precond_new = (new_residual - jnp.dot(coef_new.T, factor, precision=highest)) / noise
    res_z_new = lax.psum(jnp.sum(new_residual * precond_new, axis=1), ("row", "col"))
    beta = res_z_new / res_z
    new_direction = precond_new + beta[:, None] * direction
    return (new_solution, new_residual, new_direction)


def solution(mesh):
    placed = (
        P(None, ("row", "col")),
        P(),
        P(),
        P(None, ("row", "col")),
        P(None, ("row", "col")),
        P(None, ("row", "col")),
        P(None, ("row", "col")),
    )
    return jax.shard_map(
        local,
        mesh=mesh,
        in_specs=placed,
        out_specs=(P(None, ("row", "col")), P(None, ("row", "col")), P(None, ("row", "col"))),
        check_vma=False,
    )
```

profile of v0, /device:TPU:1, one launch (start us, length us, event | category | flops | bytes accessed | tf_op | source)
XLA Modules:
  0.0 1093.4 jit_solution(8534292449255985838)
XLA Ops:
  10.5 38.0 %all_gather.14 = f32[16,2048]{1,0:T(8,128)S(1)} all-gather(f32[16,128]{1,0:T(8,128)S(1)} %broadcast_divide_fusion), channel_id=1, replica_groups=mesh['row'=16,'col'=32] {'row'}, dimensions={1}, use_global_device_ids=true | all-gather | bytes 139264 | tf_op jit(solution)/shard_map/all_gather | solution.py:45
  48.6 64.9 %all_gather.13 = f32[16,4096]{1,0:T(8,128)S(1)} all-gather(f32[16,128]{1,0:T(8,128)S(1)} %broadcast_divide_fusion), channel_id=1, replica_groups=mesh['row'=16,'col'=32] {'col'}, dimensions={1}, use_global_device_ids=true | all-gather | bytes 270336 | tf_op jit(solution)/shard_map/all_gather | solution.py:65
  113.5 30.4 %all_gather.12 = f32[16,2048]{1,0:T(8,128)S(1)} all-gather(f32[16,128]{1,0:T(8,128)S(1)} %copy-done.3), channel_id=1, replica_groups=mesh['row'=16,'col'=32] {'row'}, dimensions={1}, use_global_device_ids=true | all-gather | bytes 139264 | tf_op jit(solution)/shard_map/all_gather | solution.py:46
  143.9 55.3 %all_gather.15 = f32[16,4096]{1,0:T(8,128)S(1)} all-gather(f32[16,128]{1,0:T(8,128)S(1)} %copy-done.3), channel_id=1, replica_groups=mesh['row'=16,'col'=32] {'col'}, dimensions={1}, use_global_device_ids=true | all-gather | bytes 270336 | tf_op jit(solution)/shard_map/all_gather | solution.py:66
  200.6 394.2 %while.14 = (s32[]{:T(128)}, f32[16,4096]{1,0:T(8,128)S(1)}, f32[16,16,128]{2,1,0:T(8,128)}, s32[16]{0:T(128)S(1)}, s32[]{:T(128)}, /*index=5*/s32[]{:T(128)}, f...) while((s32[]{:T(128)}, f32[16,4096]{1,0:T(8,128)S(1)}, ...), condition=%wide.region_11.13_spmd.clone.clone, body=%wide.region_8.12_spmd.clone.clone.sunk | while | flops 308033728 | bytes 8255933 | solution.py:104
  202.4 21.3 %conditional.4 = (f32[16,4096]{1,0:T(8,128)}, f32[1,16,128]{2,1,0:T(8,128)S(1)}) conditional(s32[]{:T(128)} %convert_element_type.21, () %tuple.92, (s32[]{:T(128)}, f32[16,2048]{1,0:T(8,128)S(1)}, f32[]{:T(128)}, f32[4096]{0:T(1024)S(1)}, f32[2048]{0:T(1024)S(1)}, /*index=5*/f32[16,2048]{1,0:T(8,128)S(1)}, f32[16,4096]{1,0:T(8,128)S(1)}, ...), branch_computations={%region_9.10_spmd, %region_10.11_spmd} | conditional | flops 307902464 | bytes 7452578 | solution.py:100
  227.0 21.3 %conditional.4 = (f32[16,4096]{1,0:T(8,128)}, f32[1,16,128]{2,1,0:T(8,128)S(1)}) conditional(s32[]{:T(128)} %convert_element_type.21, () %tuple.92, (s32[]{:T(128)}, f32[16,2048]{1,0:T(8,128)S(1)}, f32[]{:T(128)}, f32[4096]{0:T(1024)S(1)}, f32[2048]{0:T(1024)S(1)}, /*index=5*/f32[16,2048]{1,0:T(8,128)S(1)}, f32[16,4096]{1,0:T(8,128)S(1)}, ...), branch_computations={%region_9.10_spmd, %region_10.11_spmd} | conditional | flops 307902464 | bytes 7452578 | solution.py:100
  251.7 21.3 %conditional.4 = (f32[16,4096]{1,0:T(8,128)}, f32[1,16,128]{2,1,0:T(8,128)S(1)}) conditional(s32[]{:T(128)} %convert_element_type.21, () %tuple.92, (s32[]{:T(128)}, f32[16,2048]{1,0:T(8,128)S(1)}, f32[]{:T(128)}, f32[4096]{0:T(1024)S(1)}, f32[2048]{0:T(1024)S(1)}, /*index=5*/f32[16,2048]{1,0:T(8,128)S(1)}, f32[16,4096]{1,0:T(8,128)S(1)}, ...), branch_computations={%region_9.10_spmd, %region_10.11_spmd} | conditional | flops 307902464 | bytes 7452578 | solution.py:100
  276.3 21.3 %conditional.4 = (f32[16,4096]{1,0:T(8,128)}, f32[1,16,128]{2,1,0:T(8,128)S(1)}) conditional(s32[]{:T(128)} %convert_element_type.21, () %tuple.92, (s32[]{:T(128)}, f32[16,2048]{1,0:T(8,128)S(1)}, f32[]{:T(128)}, f32[4096]{0:T(1024)S(1)}, f32[2048]{0:T(1024)S(1)}, /*index=5*/f32[16,2048]{1,0:T(8,128)S(1)}, f32[16,4096]{1,0:T(8,128)S(1)}, ...), branch_computations={%region_9.10_spmd, %region_10.11_spmd} | conditional | flops 307902464 | bytes 7452578 | solution.py:100
  300.9 21.3 %conditional.4 = (f32[16,4096]{1,0:T(8,128)}, f32[1,16,128]{2,1,0:T(8,128)S(1)}) conditional(s32[]{:T(128)} %convert_element_type.21, () %tuple.92, (s32[]{:T(128)}, f32[16,2048]{1,0:T(8,128)S(1)}, f32[]{:T(128)}, f32[4096]{0:T(1024)S(1)}, f32[2048]{0:T(1024)S(1)}, /*index=5*/f32[16,2048]{1,0:T(8,128)S(1)}, f32[16,4096]{1,0:T(8,128)S(1)}, ...), branch_computations={%region_9.10_spmd, %region_10.11_spmd} | conditional | flops 307902464 | bytes 7452578 | solution.py:100
  325.6 21.3 %conditional.4 = (f32[16,4096]{1,0:T(8,128)}, f32[1,16,128]{2,1,0:T(8,128)S(1)}) conditional(s32[]{:T(128)} %convert_element_type.21, () %tuple.92, (s32[]{:T(128)}, f32[16,2048]{1,0:T(8,128)S(1)}, f32[]{:T(128)}, f32[4096]{0:T(1024)S(1)}, f32[2048]{0:T(1024)S(1)}, /*index=5*/f32[16,2048]{1,0:T(8,128)S(1)}, f32[16,4096]{1,0:T(8,128)S(1)}, ...), branch_computations={%region_9.10_spmd, %region_10.11_spmd} | conditional | flops 307902464 | bytes 7452578 | solution.py:100
  350.2 21.3 %conditional.4 = (f32[16,4096]{1,0:T(8,128)}, f32[1,16,128]{2,1,0:T(8,128)S(1)}) conditional(s32[]{:T(128)} %convert_element_type.21, () %tuple.92, (s32[]{:T(128)}, f32[16,2048]{1,0:T(8,128)S(1)}, f32[]{:T(128)}, f32[4096]{0:T(1024)S(1)}, f32[2048]{0:T(1024)S(1)}, /*index=5*/f32[16,2048]{1,0:T(8,128)S(1)}, f32[16,4096]{1,0:T(8,128)S(1)}, ...), branch_computations={%region_9.10_spmd, %region_10.11_spmd} | conditional | flops 307902464 | bytes 7452578 | solution.py:100
  374.9 21.3 %conditional.4 = (f32[16,4096]{1,0:T(8,128)}, f32[1,16,128]{2,1,0:T(8,128)S(1)}) conditional(s32[]{:T(128)} %convert_element_type.21, () %tuple.92, (s32[]{:T(128)}, f32[16,2048]{1,0:T(8,128)S(1)}, f32[]{:T(128)}, f32[4096]{0:T(1024)S(1)}, f32[2048]{0:T(1024)S(1)}, /*index=5*/f32[16,2048]{1,0:T(8,128)S(1)}, f32[16,4096]{1,0:T(8,128)S(1)}, ...), branch_computations={%region_9.10_spmd, %region_10.11_spmd} | conditional | flops 307902464 | bytes 7452578 | solution.py:100
  399.5 21.3 %conditional.4 = (f32[16,4096]{1,0:T(8,128)}, f32[1,16,128]{2,1,0:T(8,128)S(1)}) conditional(s32[]{:T(128)} %convert_element_type.21, () %tuple.92, (s32[]{:T(128)}, f32[16,2048]{1,0:T(8,128)S(1)}, f32[]{:T(128)}, f32[4096]{0:T(1024)S(1)}, f32[2048]{0:T(1024)S(1)}, /*index=5*/f32[16,2048]{1,0:T(8,128)S(1)}, f32[16,4096]{1,0:T(8,128)S(1)}, ...), branch_computations={%region_9.10_spmd, %region_10.11_spmd} | conditional | flops 307902464 | bytes 7452578 | solution.py:100
  424.1 21.3 %conditional.4 = (f32[16,4096]{1,0:T(8,128)}, f32[1,16,128]{2,1,0:T(8,128)S(1)}) conditional(s32[]{:T(128)} %convert_element_type.21, () %tuple.92, (s32[]{:T(128)}, f32[16,2048]{1,0:T(8,128)S(1)}, f32[]{:T(128)}, f32[4096]{0:T(1024)S(1)}, f32[2048]{0:T(1024)S(1)}, /*index=5*/f32[16,2048]{1,0:T(8,128)S(1)}, f32[16,4096]{1,0:T(8,128)S(1)}, ...), branch_computations={%region_9.10_spmd, %region_10.11_spmd} | conditional | flops 307902464 | bytes 7452578 | solution.py:100
  426.0 1.2 exponential_multiply_fusion.6
  448.8 21.3 %conditional.4 = (f32[16,4096]{1,0:T(8,128)}, f32[1,16,128]{2,1,0:T(8,128)S(1)}) conditional(s32[]{:T(128)} %convert_element_type.21, () %tuple.92, (s32[]{:T(128)}, f32[16,2048]{1,0:T(8,128)S(1)}, f32[]{:T(128)}, f32[4096]{0:T(1024)S(1)}, f32[2048]{0:T(1024)S(1)}, /*index=5*/f32[16,2048]{1,0:T(8,128)S(1)}, f32[16,4096]{1,0:T(8,128)S(1)}, ...), branch_computations={%region_9.10_spmd, %region_10.11_spmd} | conditional | flops 307902464 | bytes 7452578 | solution.py:100
  473.4 21.3 %conditional.4 = (f32[16,4096]{1,0:T(8,128)}, f32[1,16,128]{2,1,0:T(8,128)S(1)}) conditional(s32[]{:T(128)} %convert_element_type.21, () %tuple.92, (s32[]{:T(128)}, f32[16,2048]{1,0:T(8,128)S(1)}, f32[]{:T(128)}, f32[4096]{0:T(1024)S(1)}, f32[2048]{0:T(1024)S(1)}, /*index=5*/f32[16,2048]{1,0:T(8,128)S(1)}, f32[16,4096]{1,0:T(8,128)S(1)}, ...), branch_computations={%region_9.10_spmd, %region_10.11_spmd} | conditional | flops 307902464 | bytes 7452578 | solution.py:100
  498.0 21.3 %conditional.4 = (f32[16,4096]{1,0:T(8,128)}, f32[1,16,128]{2,1,0:T(8,128)S(1)}) conditional(s32[]{:T(128)} %convert_element_type.21, () %tuple.92, (s32[]{:T(128)}, f32[16,2048]{1,0:T(8,128)S(1)}, f32[]{:T(128)}, f32[4096]{0:T(1024)S(1)}, f32[2048]{0:T(1024)S(1)}, /*index=5*/f32[16,2048]{1,0:T(8,128)S(1)}, f32[16,4096]{1,0:T(8,128)S(1)}, ...), branch_computations={%region_9.10_spmd, %region_10.11_spmd} | conditional | flops 307902464 | bytes 7452578 | solution.py:100
  522.7 21.3 %conditional.4 = (f32[16,4096]{1,0:T(8,128)}, f32[1,16,128]{2,1,0:T(8,128)S(1)}) conditional(s32[]{:T(128)} %convert_element_type.21, () %tuple.92, (s32[]{:T(128)}, f32[16,2048]{1,0:T(8,128)S(1)}, f32[]{:T(128)}, f32[4096]{0:T(1024)S(1)}, f32[2048]{0:T(1024)S(1)}, /*index=5*/f32[16,2048]{1,0:T(8,128)S(1)}, f32[16,4096]{1,0:T(8,128)S(1)}, ...), branch_computations={%region_9.10_spmd, %region_10.11_spmd} | conditional | flops 307902464 | bytes 7452578 | solution.py:100
  547.3 21.3 %conditional.4 = (f32[16,4096]{1,0:T(8,128)}, f32[1,16,128]{2,1,0:T(8,128)S(1)}) conditional(s32[]{:T(128)} %convert_element_type.21, () %tuple.92, (s32[]{:T(128)}, f32[16,2048]{1,0:T(8,128)S(1)}, f32[]{:T(128)}, f32[4096]{0:T(1024)S(1)}, f32[2048]{0:T(1024)S(1)}, /*index=5*/f32[16,2048]{1,0:T(8,128)S(1)}, f32[16,4096]{1,0:T(8,128)S(1)}, ...), branch_computations={%region_9.10_spmd, %region_10.11_spmd} | conditional | flops 307902464 | bytes 7452578 | solution.py:100
  572.0 21.3 %conditional.4 = (f32[16,4096]{1,0:T(8,128)}, f32[1,16,128]{2,1,0:T(8,128)S(1)}) conditional(s32[]{:T(128)} %convert_element_type.21, () %tuple.92, (s32[]{:T(128)}, f32[16,2048]{1,0:T(8,128)S(1)}, f32[]{:T(128)}, f32[4096]{0:T(1024)S(1)}, f32[2048]{0:T(1024)S(1)}, /*index=5*/f32[16,2048]{1,0:T(8,128)S(1)}, f32[16,4096]{1,0:T(8,128)S(1)}, ...), branch_computations={%region_9.10_spmd, %region_10.11_spmd} | conditional | flops 307902464 | bytes 7452578 | solution.py:100
  595.9 98.1 %psum.43 = f32[128,16]{1,0:T(8,128)S(1)} all-reduce(f32[128,16]{1,0:T(8,128)S(1)} %fusion.120), channel_id=1, replica_groups=mesh['row'=16,'col'=32] {'row','col'}, use_global_device_ids=true, to_apply=%region_3.4 | all-reduce | flops 2048 | bytes 16384 | tf_op jit(solution)/shard_map/psum | solution.py:52
  694.0 1.5 select_add_fusion.1
  697.0 11.7 %cholesky.19 = f32[128,128]{1,0:T(8,128)S(1)} custom-call(f32[128,128]{1,0:T(8,128)S(1)} %fusion.113), custom_call_target="Cholesky" | custom-call | tf_op jit(solution)/shard_map/jit(cholesky)/cholesky | solution.py:53
  710.0 9.8 custom-call.10
  721.4 57.9 %reduce-scatter.3.cloned.1.call-done = f32[16,128]{1,0:T(8,128)} async-done(((f32[16,4096]{1,0:T(8,128)}), f32[16,128]{1,0:T(8,128)}) %reduce-scatter.3.cloned.1.call-update) | async-done | bytes 8208 | tf_op jit(solution)/shard_map/reduce_scatter | solution.py:105
  779.3 1.5 multiply_reduce_fusion.3
  780.8 101.8 %all-reduce = (f32[16]{0:T(128)S(1)}, f32[16]{0:T(128)S(1)}) all-reduce(f32[16]{0:T(128)S(1)} %fusion.103, f32[16]{0:T(128)S(1)} %multiply_reduce_fusion.3), channel_id=1, replica_groups=mesh['row'=16,'col'=32] {'row','col'}, use_global_device_ids=true, to_apply=%region_5.7 | all-reduce | flops 32 | bytes 256 | tf_op jit(solution)/shard_map/psum | solution.py:108
  882.6 1.3 multiply_subtract_fusion
  884.1 100.3 %psum.46 = f32[128,16]{0,1:T(8,128)S(1)} all-reduce(f32[128,16]{0,1:T(8,128)S(1)} %convolution_bitcast_fusion), channel_id=1, replica_groups=mesh['row'=16,'col'=32] {'row','col'}, use_global_device_ids=true, to_apply=%region_16.18 | all-reduce | flops 2048 | bytes 16384 | tf_op jit(solution)/shard_map/psum | solution.py:112
  985.8 99.4 %psum.47 = f32[16]{0:T(128)S(1)} all-reduce(f32[16]{0:T(128)S(1)} %get-tuple-element.374), channel_id=1, replica_groups=mesh['row'=16,'col'=32] {'row','col'}, use_global_device_ids=true, to_apply=%region_18.20 | all-reduce | flops 16 | bytes 128 | tf_op jit(solution)/shard_map/psum | solution.py:115
  (807 shorter events, 372.1 us)
Async XLA Ops:
  8.0 0.8 copy-start
  8.0 686.0 %all-reduce.3.cloned.1.call-start = ((), (), s32[]{:S(2)}) async-start(), calls=%async_computation.2 | async-start | bytes 131072 | tf_op jit(solution)/shard_map/psum | solution.py:52
  9.7 0.7 copy-start.9
  9.8 711.6 %reduce-scatter.5.cloned.1.call-start = ((), (), s32[]{:S(2)}) async-start(), calls=%async_computation.4 | async-start | bytes 139264 | tf_op jit(solution)/shard_map/reduce_scatter | solution.py:106
  9.8 0.7 copy-start.11
  48.6 64.9 %copy-start.3 = (f32[16,128]{1,0:T(8,128)S(1)}, f32[16,128]{1,0:T(8,128)}, u32[]{:S(2)}) copy-start(f32[16,128]{1,0:T(8,128)} %param.19) | copy-start | bytes 24580
  199.2 0.7 copy-start.10
  594.8 0.7 copy-start.1
  594.9 184.4 %reduce-scatter.3.cloned.1.call-start = ((), (), s32[]{:S(2)}) async-start(), calls=%async_computation.3 | async-start | bytes 270336 | tf_op jit(solution)/shard_map/reduce_scatter | solution.py:105
  594.9 0.7 copy-start.4
  695.5 0.8 copy-start.2
  779.3 103.3 %copy-start.6 = (f32[1,16,128]{2,1,0:T(8,128)S(1)}, f32[1,16,128]{2,1,0:T(8,128)}, u32[]{:S(2)}) copy-start(f32[1,16,128]{2,1,0:T(8,128)} %reduce-scatter.5.cloned.1.call-done) | copy-start | bytes 24580
  779.3 103.3 %copy-start.7 = (f32[16,128]{1,0:T(8,128)S(1)}, f32[16,128]{1,0:T(8,128)}, u32[]{:S(2)}) copy-start(f32[16,128]{1,0:T(8,128)} %reduce-scatter.3.cloned.1.call-done) | copy-start | bytes 24580
  779.3 103.3 %copy-start.8 = (f32[16,128]{1,0:T(8,128)S(1)}, f32[16,128]{1,0:T(8,128)}, u32[]{:S(2)}) copy-start(f32[16,128]{1,0:T(8,128)} %param.17) | copy-start | bytes 24580
  883.9 100.9 %copy-start.5 = (f32[16,128]{1,0:T(8,128)}, f32[16,128]{1,0:T(8,128)S(1)}, u32[]{:S(2)}) copy-start(f32[16,128]{1,0:T(8,128)S(1)} %get-tuple-element.370) | copy-start | bytes 24580
Sparse Core Ops, SparseCore 0:
  14.3 448.2 all-reduce.2
Sparse Core Ops, SparseCore 1:
  595.0 66.3 reduce-scatter.4
  665.5 113.7 reduce-scatter.2
where the time goes:
time: 1100 us; the launch traced here: 1090 us
  blocking collectives  588 us (53%)
  matrix products  310 us (28%)
  waiting for transfers between devices  58 us (5%)
  other arithmetic  45.2 us (4%)
  local copies, waits for them, and re-layouts  43.4 us (4%)
  loops' own time  32.4 us (3%)
  between operations  15.7 us (1%)
    dot_general x128, matrix products, pair_terms(): lax.dot_general(block_pts, right_pts, (((0,), (0,)), ((), ())), precision...  158 us
    dot_general x128, matrix products, pair_terms(): lax.dot_general(right_dir, kernel, (((1,), (1,)), ((), ())), precision=hi...  113 us
    psum x1, blocking collectives, local(): lax.psum((first_local, jnp.sum(direction * image, axis=1)), ('row', 'col'))  102 us
    psum x1, blocking collectives, local(): lax.psum(jnp.dot(new_residual, factor.T, precision=highest), ('row', 'col'))  100 us
    psum x1, blocking collectives, local(): lax.psum(jnp.sum(new_residual * precond_new, axis=1), ('row', 'col'))  99.4 us
    psum x1, blocking collectives, local(): gram, proj_res = lax.psum((gram_local, proj_local), ('row', 'col'))  98.1 us
    all_gather x1, blocking collectives, local(): lax.all_gather(scaled, 'col', axis=1, tiled=True)  64.9 us
    reduce_scatter x1, waiting for transfers between devices, local(): row_sum = lax.psum_scatter(acc, 'col', scatter_dimension=1, tiled=True)  57.9 us
  transfers between devices with their start and end apart: 3, of which 1 were waited for; matrix products, arithmetic and copies ran while one was open for 36% of the time, Pallas kernels for 0%

commit v1 on v0

v1 whole, which is shorter than its diff:
```python
import functools
import math

import jax
import jax.numpy as jnp
from jax import lax
from jax.experimental import pallas as pl
from jax.experimental.pallas import tpu as pltpu
from jax.sharding import PartitionSpec as P

F32 = jnp.float32
BF16 = jnp.bfloat16
MESH = pl.DeviceIdType.MESH
highest = lax.Precision.HIGHEST
NT = (((1,), (1,)), ((), ()))
X, Y, Z_HI, Z_LO = 4, 4, 4, 4
LN2 = math.log(2.0)
SCALE = math.sqrt(5.0) / LN2
POLY = LN2 * LN2 / 3.0
POLY_A = 3.0 / LN2
POLY_B = 3.0 / (LN2 * LN2)


def div(a, b):
    return a // b if isinstance(a, int) else lax.div(a, jnp.int32(b))


def rem(a, b):
    return a % b if isinstance(a, int) else lax.rem(a, jnp.int32(b))


def lanes(start, size):
    if isinstance(start, int):
        return slice(start, start + size)
    return pl.ds(pl.multiple_of(start, 128), size)


def split2(v):
    hi = v.astype(BF16)
    return hi, (v - hi.astype(F32)).astype(BF16)


def split3(v):
    hi = v.astype(BF16)
    left = v - hi.astype(F32)
    mid = left.astype(BF16)
    return hi, mid, (left - mid.astype(F32)).astype(BF16)


def matern(t_sq):
    t_sq = jnp.maximum(t_sq, 1e-30)
    t = t_sq * lax.rsqrt(t_sq)
    return (t * (t + POLY_A) + POLY_B) * jnp.exp2(-t)


def dot(a, b):
    return jnp.dot(a, b, preferred_element_type=F32)


def dot_nt(a, b):
    return lax.dot_general(a, b, NT, preferred_element_type=F32)


def shifts_of(nz):
    full = [d if d % 2 else -d for d in range(2, nz // 2)]
    pairs = [(full[i], full[i + 1]) for i in range(0, len(full), 2)]
    if len(pairs) > 1:
        pairs = [pairs[0]] + pairs[:0:-1]
    return pairs, nz // 2, 1


def kernel(
    points_ref, ls_ref, var_ref, factor_ref, solution_ref, residual_ref, direction_ref,
    sol_out, res_out, dir_out,
    item, items, zitems, a_mat, dp, bt, dq, btf, dqf,
    t_a, t_b, h_a, h_b, l_a, l_b, ft_a, ft_b, fh_a, fh_b, fl_a, fl_b,
    left, right, right_f, lsend, lrx, rsend, rrx,
    g_send, g_rx, g_piece, g_px, g_tot, g_all, core_ref,
    v_send, v_rx, v_piece, v_px, v_tot, v_all, projres_ref,
    send_sem, recv_sem,
):
    nz, npl = Z_HI * Z_LO, X * Y * 2
    tp = npl // 2
    pairs, half_shift, single = shifts_of(nz)
    probes = direction_ref.shape[0]
    row, col = lax.axis_index("row"), lax.axis_index("col")
    z = rem(div(col, 2), Z_HI) * Z_LO + div(row, Y)
    s = (div(col, 2 * Z_HI) * Y + rem(row, Y)) * 2 + rem(col, 2)

    def device(zz, ss):
        r = rem(zz, Z_LO) * Y + rem(div(ss, 2), Y)
        c = div(ss, 2 * Y) * (2 * Z_HI) + div(zz, Z_LO) * 2 + rem(ss, 2)
        return (r, c)

    def in_plane(j):
        return device(z, rem(s + j + npl, npl))

    def in_column(i):
        return device(rem(z + i + nz, nz), s)

    def send(kind, src, dst, target):
        pltpu.make_async_remote_copy(
            src_ref=src, dst_ref=dst, send_sem=send_sem.at[kind], recv_sem=recv_sem.at[kind],
            device_id=target, device_id_type=MESH,
        ).start()

    def wait(sem, kind, ref):
        pltpu.make_async_copy(ref, ref, sem.at[kind]).wait()

    def loop(lo, hi, body):
        def step(i, carry):
            body(i)
            return carry

        lax.fori_loop(lo, hi, step, 0)

    barrier = pltpu.get_barrier_semaphore()
    loop(1, npl, lambda j: pl.semaphore_signal(barrier, inc=1, device_id=in_plane(j), device_id_type=MESH))
    loop(1, nz, lambda i: pl.semaphore_signal(barrier, inc=1, device_id=in_column(i), device_id_type=MESH))

    sub16 = lax.broadcasted_iota(jnp.int32, (16, 128), 0)
    lane16 = lax.broadcasted_iota(jnp.int32, (16, 128), 1)
    scale = jnp.zeros((16, 128), F32)
    for i in range(16):
        scale = jnp.where(sub16 == i, ls_ref[i], scale)
    direction = direction_ref[...]
    residual = residual_ref[...]
    noise = var_ref[1]
    item[0:16, :] = (points_ref[...] - 0.5) / scale * SCALE
    item[16:32, :] = direction
    pl.semaphore_wait(barrier, npl + nz - 2)

    loop(1, npl, lambda j: send(0, item, items.at[j], in_plane(j)))
    shifts = [d for p in pairs for d in p] + [half_shift, single]
    slot_of = {d: i for i, d in enumerate(shifts)}
    z_order = sorted(shifts, key=lambda d: (d not in pairs[0] if pairs else False, abs(d)))
    for d in z_order:
        i = slot_of[d]
        pltpu.make_async_remote_copy(
            src_ref=item, dst_ref=zitems.at[i], send_sem=send_sem.at[1], recv_sem=recv_sem.at[10 + i],
            device_id=in_column(-d), device_id_type=MESH,
        ).start()

    factor = factor_ref[...]
    gram = lax.dot_general(factor, factor, NT, precision=highest, preferred_element_type=F32)
    g_send[...] = gram.reshape(g_send.shape)
    projres_ref[...] = lax.dot_general(residual, factor, NT, precision=highest, preferred_element_type=F32)
    loop(1, nz, lambda i: send(2, g_send.at[rem(z + i, nz)], g_rx.at[i], in_column(i)))

    def pieces(item_val):
        u, d = item_val[0:16], item_val[16:32]
        sq = jnp.sum(u * u, axis=0, keepdims=True)
        return split3(u), [v.astype(F32) for v in split3(sq)], split2(d)

    def tail(sq, first):
        out = jnp.zeros((16, 128), F32)
        for i in range(3):
            out = jnp.where(sub16 == first + i, sq[i], out)
        return jnp.where((sub16 >= 3 - first) & (sub16 < 6 - first), 1.0, out)

    def build_a(slot, item_val):
        (hi, mid, lo), sq, (dhi, dlo) = pieces(item_val)
        at = lanes(slot * 128, 128)
        for g, v in enumerate((hi, hi, mid, hi, lo, mid, tail(sq, 0).astype(BF16))):
            a_mat[g * 16 : g * 16 + 16, at] = v
        a_mat[112:128, at] = jnp.zeros((16, 128), BF16)
        dp[0:16, at] = dhi
        dp[16:32, at] = dlo

    def build_b(item_val):
        (hi, mid, lo), sq, (dhi, dlo) = pieces(item_val)
        hi, mid, lo = (-2.0 * v.astype(F32) for v in (hi, mid, lo))
        wide = jnp.concatenate([hi, mid, hi, lo, hi, mid, tail(sq, 3), jnp.zeros((16, 128), F32)], axis=0)
        return wide.T.astype(BF16), jnp.concatenate([dhi, dlo], axis=0)

    own = item[...]
    build_a(0, own)
    build_a(npl, own)
    b, d_b = build_b(own)
    bt[1, 0:128, :] = b
    dq[1, :, 0:128] = d_b
    right[...] = jnp.zeros_like(right)
    right_f[...] = jnp.zeros_like(right_f)
    left[1] = jnp.zeros(left.shape[1:], F32)

    def take_z(d, store):
        i = slot_of[d]
        wait(recv_sem, 10 + i, zitems.at[i])
        store(build_b(zitems[i]))

    def into(qt, half):
        def store(bd):
            bt[qt, half * 128 : half * 128 + 128, :] = bd[0]
            dq[qt, :, half * 128 : half * 128 + 128] = bd[1]

        return store

    def into_f(bd):
        btf[...] = bd[0]
        dqf[...] = bd[1]

    wait(recv_sem, 0, items.at[pl.ds(1, npl - 1)])
    loop(1, npl, lambda j: build_a(j, items[j]))

    def place(k):
        kk = k + (tp // 2) * div(k + 64 - 3 * tp // 2, 64)
        return div(kk, tp), rem(kk, tp)

    bufs = ((t_a, h_a, l_a), (t_b, h_b, l_b))

    def cross(k, par):
        qt, pt = place(k)
        bufs[par][0][...] = dot(bt[qt], a_mat[:, lanes(pt * 256, 256)])

    def elementwise(par):
        t, h, l = bufs[par]
        h[...], l[...] = split2(matern(t[...]))

    def apply(k, par):
        qt, pt = place(k)
        _, h, l = bufs[par]
        at = lanes(pt * 256, 256)
        d_q, d_p = dq[qt], dp[:, at]
        hi, lo = h[...], l[...]
        left[qt, :, at] = dot(d_q, hi) + dot(d_q, lo)
        right[qt] += dot_nt(d_p, hi) + dot_nt(d_p, lo)

    def steps(first, last):
        def one(k, par):
            apply(k - 2, par)
            elementwise(1 - par)
            cross(k, par)

        k = first
        if first == 0:
            cross(0, 0)
            elementwise(0)
            if last > 1:
                cross(1, 1)
            k = min(2, last)
        if (last - k) % 2 == 0 and last - k >= 4:

            def two(i):
                one(2 * i, 0)
                one(2 * i + 1, 1)

            loop(k // 2, last // 2, two)
        else:
            for kk in range(k, last):
                one(kk, kk % 2)

    def send_right(qt, halves):
        both = right[qt, 0:16, :] + right[qt, 16:32, :]
        for h, d in halves:
            i = slot_of[d]
            rsend[i] = both[:, h * 128 : h * 128 + 128]
            send(3, rsend.at[i], rrx.at[i], in_column(d))

    def gram_stage(stage):
        if stage == 0:
            wait(recv_sem, 2, g_rx.at[pl.ds(1, nz - 1)])
            total = g_send[z]
            for i in range(1, nz):
                total = total + g_rx[i]
            g_piece[...] = total
            loop(1, npl, lambda j: send(4, g_piece, g_px.at[j], in_plane(j)))
        elif stage == 1:
            wait(recv_sem, 4, g_px.at[pl.ds(1, npl - 1)])
            total = g_piece[...]
            for j in range(1, npl):
                total = total + g_px[j]
            g_tot[...] = total
            g_all[z] = total
            loop(1, nz, lambda i: send(5, g_tot, g_all.at[z], in_column(i)))
        else:
            wait(recv_sem, 5, g_rx.at[pl.ds(1, nz - 1)])
            eye = lax.broadcasted_iota(jnp.int32, (128, 128), 0) == lax.broadcasted_iota(jnp.int32, (128, 128), 1)
            core_ref[...] = g_all[...].reshape(128, 128) + jnp.where(eye, noise, 0.0)

    lane128 = lax.broadcasted_iota(jnp.int32, (128, 128), 1)
    sub128 = lax.broadcasted_iota(jnp.int32, (128, 128), 0)

    def sweep(k):
        m = core_ref[...]
        line = core_ref[pl.ds(k, 1), :]
        column = jnp.sum(jnp.where(lane128 == k, m, 0.0), axis=1, keepdims=True)
        pivot = jnp.sum(jnp.where(lane128[0:1] == k, line, 0.0), axis=1, keepdims=True)
        inv = 1.0 / pivot
        line = line * inv
        new = jnp.where(sub128 == k, line, m - column * line)
        core_ref[...] = jnp.where(lane128 == k, jnp.where(sub128 == k, -inv, column * inv), new)

    if pairs:
        take_z(pairs[0][0], into(0, 0))
        take_z(pairs[0][1], into(0, 1))
    steps(0, tp)
    gram_stage(0)
    take_z(half_shift, into(1, 1))
    steps(tp, tp + tp // 2)
    if pairs:
        send_right(0, ((0, pairs[0][0]), (1, pairs[0][1])))
    middle = lanes(tp * 128, 128)
    hi, lo = split2(matern(dot(bt[1], a_mat[:, middle])))
    d_p = dp[:, middle]
    right[1] += dot_nt(d_p, hi) + dot_nt(d_p, lo)
    gram_stage(1)
    end = tp + tp // 2
    for n, pair in enumerate(pairs[1:]):
        take_z(pair[0], into(2 + n, 0))
        take_z(pair[1], into(2 + n, 1))
        steps(end, end + tp)
        end += tp
        if n == 0:
            send_right(1, ((1, half_shift),))
        else:
            send_right(1 + n, ((0, pairs[n][0]), (1, pairs[n][1])))
    take_z(single, into_f)
    elementwise((end - 1) % 2)
    apply(end - 2, end % 2)
    apply(end - 1, (end - 1) % 2)
    if len(pairs) > 1:
        send_right(len(pairs), ((0, pairs[-1][0]), (1, pairs[-1][1])))
    else:
        send_right(1, ((1, half_shift),))
    gram_stage(2)

    fbufs = ((ft_a, fh_a, fl_a), (ft_b, fh_b, fl_b))

    def f_cross(k, par):
        fbufs[par][0][...] = dot(btf[...], a_mat[:, lanes(k * 512 + 128, 512)])

    def f_elementwise(par):
        t, h, l = fbufs[par]
        h[...], l[...] = split2(matern(t[...]))

    def f_apply(k, par, last=False):
        _, h, l = fbufs[par]
        d_q, d_p = dqf[...], dp[:, lanes(k * 512 + 128, 512)]
        hi, lo = h[...], l[...]
        out = dot(d_q, hi) + dot(d_q, lo)
        right_f[...] += dot_nt(d_p, hi) + dot_nt(d_p, lo)
        for i in range(4):
            j = k * 4 + 1 + i
            mine = last and i == 3
            total = out[0:16, i * 128 : i * 128 + 128] + out[16:32, i * 128 : i * 128 + 128]
            at = slice(0, 128) if mine else lanes(j * 128, 128)
            for qt in range(left.shape[0]):
                if not (mine and qt == 1) and not (qt == 0 and not pairs):
                    total = total + (left[qt, 0:16, at] + left[qt, 16:32, at])
            lsend[j] = total
            if not mine:
                send(6, lsend.at[j], lrx.at[npl - j], in_plane(-j))

    count = npl // 4

    def f_one(k, par):
        f_apply(k - 2, par)
        f_elementwise(1 - par)
        f_cross(k, par)

    f_cross(0, 0)
    f_elementwise(0)
    if count > 1:
        f_cross(1, 1)

        def f_two(i):
            f_one(2 * i, 0)
            f_one(2 * i + 1, 1)

        loop(1, count // 2, f_two)
        f_elementwise((count - 1) % 2)
        f_apply(count - 2, count % 2)
    f_apply(count - 1, (count - 1) % 2, last=True)
    i = slot_of[single]
    rsend[i] = right_f[0:16, :] + right_f[16:32, :]
    send(3, rsend.at[i], rrx.at[i], in_column(single))

    loop(0, 64, sweep)

    wait(recv_sem, 6, lrx.at[pl.ds(1, npl - 1)])
    wait(recv_sem, 3, rrx)
    total = lsend[npl] + (right[1, 0:16, 0:128] + right[1, 16:32, 0:128])
    for j in range(1, npl):
        total = total + lrx[j]
    for i in range(len(shifts)):
        total = total + rrx[i]
    image = (var_ref[0] * POLY) * total + noise * direction

    proj_im = lax.dot_general(image, factor, NT, precision=highest, preferred_element_type=F32)
    proj_re = projres_ref[...]
    scalars = jnp.zeros((16, 128), F32)
    for n, (a, b) in enumerate(((direction, image), (residual, image), (image, image), (residual, residual))):
        scalars = jnp.where(lane16 == n, jnp.sum(a * b, axis=1, keepdims=True), scalars)
    per = probes // nz
    for p in range(probes):
        for n, v in enumerate((proj_im, proj_re, scalars)):
            at = (p % per) * 4 + n
            v_send[p // per, at : at + 1, :] = v[p : p + 1, :]
        at = (p % per) * 4 + 3
        v_send[p // per, at : at + 1, :] = jnp.zeros((1, 128), F32)
    loop(1, nz, lambda i: send(7, v_send.at[rem(z + i, nz)], v_rx.at[i], in_column(i)))
    loop(64, 96, sweep)
    wait(recv_sem, 7, v_rx.at[pl.ds(1, nz - 1)])
    total = v_send[z]
    for i in range(1, nz):
        total = total + v_rx[i]
    v_piece[...] = total
    loop(1, npl, lambda j: send(8, v_piece, v_px.at[j], in_plane(j)))
    loop(96, 128, sweep)
    wait(recv_sem, 8, v_px.at[pl.ds(1, npl - 1)])
    total = v_piece[...]
    for j in range(1, npl):
        total = total + v_px[j]
    v_tot[...] = total
    v_all[z] = total
    loop(1, nz, lambda i: send(9, v_tot, v_all.at[z], in_column(i)))
    core_inv = -core_ref[...]
    wait(recv_sem, 9, v_rx.at[pl.ds(1, nz - 1)])

    def gathered(n):
        out = jnp.zeros((16, 128), F32)
        for p in range(probes):
            at = (p % per) * 4 + n
            out = jnp.where(sub16 == p, v_all[p // per, at : at + 1, :], out)
        return out

    proj_im, proj_re, scalars = gathered(0), gathered(1), gathered(2)
    d_im, r_im, im_im, r_r = (scalars[:, n : n + 1] for n in range(4))
    both = jnp.dot(
        jnp.concatenate([proj_re, proj_im], axis=0), core_inv, precision=highest, preferred_element_type=F32
    )
    coef_re, coef_im = both[0:16], both[16:32]
    res_z = (r_r - jnp.sum(proj_re * coef_re, axis=1, keepdims=True)) / noise
    alpha = res_z / d_im
    coef_new = coef_re - alpha * coef_im
    proj_new = proj_re - alpha * proj_im
    new_sq = r_r - 2.0 * alpha * r_im + alpha * alpha * im_im
    res_z_new = (new_sq - jnp.sum(proj_new * coef_new, axis=1, keepdims=True)) / noise
    beta = res_z_new / res_z
    new_residual = residual - alpha * image
    sol_out[...] = solution_ref[...] + alpha * direction
    res_out[...] = new_residual
    fitted = jnp.dot(coef_new, factor, precision=highest, preferred_element_type=F32)
    dir_out[...] = (new_residual - fitted) / noise + beta * direction

    wait(send_sem, 0, items.at[pl.ds(1, npl - 1)])
    wait(send_sem, 1, zitems)
    wait(send_sem, 2, g_rx.at[pl.ds(1, nz - 1)])
    wait(send_sem, 3, rrx)
    wait(send_sem, 4, g_px.at[pl.ds(1, npl - 1)])
    wait(send_sem, 5, g_rx.at[pl.ds(1, nz - 1)])
    wait(send_sem, 6, lrx.at[pl.ds(1, npl - 1)])
    wait(send_sem, 7, v_rx.at[pl.ds(1, nz - 1)])
    wait(send_sem, 8, v_px.at[pl.ds(1, npl - 1)])
    wait(send_sem, 9, v_rx.at[pl.ds(1, nz - 1)])


def local(points, lengthscales, variances, factor, solution, residual, direction):
    nz, npl = Z_HI * Z_LO, X * Y * 2
    pairs, _, _ = shifts_of(nz)
    blocks = 2 * len(pairs) + 2
    nq = 2 + max(len(pairs) - 1, 0)
    gr, vr = 128 // nz, 4 * (16 // nz)
    wide = (npl + 1) * 128
    vmem = pl.BlockSpec(memory_space=pltpu.VMEM)
    smem = pl.BlockSpec(memory_space=pltpu.SMEM)
    tile, ftile = (256, 256), (128, 512)
    scratch = [
        ((32, 128), F32), ((npl, 32, 128), F32), ((blocks, 32, 128), F32),
        ((128, wide), BF16), ((32, wide), BF16), ((nq, 256, 128), BF16), ((nq, 32, 256), BF16),
        ((128, 128), BF16), ((32, 128), BF16),
        (tile, F32), (tile, F32), (tile, BF16), (tile, BF16), (tile, BF16), (tile, BF16),
        (ftile, F32), (ftile, F32), (ftile, BF16), (ftile, BF16), (ftile, BF16), (ftile, BF16),
        ((nq, 32, npl * 128), F32), ((nq, 32, 256), F32), ((32, 128), F32),
        ((npl + 1, 16, 128), F32), ((npl, 16, 128), F32), ((blocks, 16, 128), F32), ((blocks, 16, 128), F32),
        ((nz, gr, 128), F32), ((nz, gr, 128), F32), ((gr, 128), F32), ((npl, gr, 128), F32),
        ((gr, 128), F32), ((nz, gr, 128), F32), ((128, 128), F32),
        ((nz, vr, 128), F32), ((nz, vr, 128), F32), ((vr, 128), F32), ((npl, vr, 128), F32),
        ((vr, 128), F32), ((nz, vr, 128), F32), ((16, 128), F32),
    ]
    out = jax.ShapeDtypeStruct(direction.shape, F32)
    return pl.pallas_call(
        kernel,
        out_shape=(out, out, out),
        in_specs=[vmem, smem, smem, vmem, vmem, vmem, vmem],
        out_specs=(vmem, vmem, vmem),
        scratch_shapes=[pltpu.VMEM(shape, dtype) for shape, dtype in scratch]
        + [pltpu.SemaphoreType.DMA((10,)), pltpu.SemaphoreType.DMA((10 + blocks,))],
        compiler_params=pltpu.CompilerParams(
            collective_id=0, has_side_effects=True, vmem_limit_bytes=40 * 2**20
        ),
    )(points, lengthscales, variances, factor, solution, residual, direction)


def solution(mesh):
    placed = P(None, ("row", "col"))
    return jax.shard_map(
        local,
        mesh=mesh,
        in_specs=(placed, P(), P(), placed, placed, placed, placed),
        out_specs=(placed, placed, placed),
        check_vma=False,
    )
```

time: 1100 us -> 85.6 us (0.08)
  blocking collectives: 588 us -> 0 us
  matrix products: 310 us -> 0 us
  Pallas kernels: 0 us -> 77.8 us
  waiting for transfers between devices: 58 us -> 0 us
  other arithmetic: 45.2 us -> 0 us
  local copies, waits for them, and re-layouts: 43.4 us -> 6.72 us
  loops' own time: 32.4 us -> 0 us
  between operations: 15.7 us -> 0.66 us
    psum x4 -> x0, blocking collectives: 400 us -> none  [the longest x1 102 us: local(): lax.psum((first_local, jnp.sum(direction * image, axis=1)), ('row', 'col'))]
    dot_general x389 -> x0, matrix products: 309 us -> none  [the longest x128 158 us: pair_terms(): lax.dot_general(block_pts, right_pts, (((0,), (0,)), ((), ())), precision...]
    all_gather x4 -> x0, blocking collectives: 189 us -> none  [the longest x1 64.9 us: local(): lax.all_gather(scaled, 'col', axis=1, tiled=True)]
    pallas_call x0 -> x1, Pallas kernels: none -> 77.8 us  [local(): pl.pallas_call(kernel, out_shape=(out, out, out), in_specs=[vmem, smem, s...]
    reduce_scatter x2 -> x0, waiting for transfers between devices: 57.9 us -> none  [the longest x1 57.9 us: local(): row_sum = lax.psum_scatter(acc, 'col', scatter_dimension=1, tiled=True)]
    another operation x17 -> x0, loops' own time: 32.4 us -> none  [the longest x1 18.5 us: local(): lax.scan(upper_step, start, jnp.arange(row_count, dtype=jnp.int32))]
    another operation x5 -> x0, other arithmetic: 22.9 us -> none  [the longest x3 12.4 us: local(): chol = jnp.linalg.cholesky(gram + noise * eye_rank)]
    slice x289 -> x0, local copies, waits for them, and re-layouts: 19.7 us -> none  [the longest x144 10.1 us: pair_terms(): right_weight[None, start:start + piece]]
  transfers between devices with their start and end apart: 3 -> 0, of which waited for: 1 -> 0; matrix products, arithmetic and copies ran while one was open for 36% -> 0% of each run, Pallas kernels for 0% -> 0%
where the time goes in v1:
time: 85.6 us; the launch traced here: 85.2 us
  Pallas kernels  77.8 us (91%)
  local copies, waits for them, and re-layouts  6.72 us (8%)
    pallas_call x1, Pallas kernels, local(): pl.pallas_call(kernel, out_shape=(out, out, out), in_specs=[vmem, smem, s...  77.8 us
    unnamed x17, local copies, waits for them, and re-layouts  6.72 us

profile of v1, /device:TPU:1, one launch (start us, length us, event | category | flops | bytes accessed | tf_op | source)
XLA Modules:
  0.0 85.2 jit_solution(12739773294530917692)
XLA Ops:
  0.6 0.0 copy-start
  0.6 0.8 copy-done
  1.5 0.0 copy-start.1
  1.5 0.7 copy-done.1
  2.2 0.0 copy-start.2
  2.2 0.7 copy-done.2
  2.9 0.0 copy-start.3
  2.9 0.7 copy-done.3
  3.6 0.0 copy-start.4
  3.6 0.7 copy-done.4
  4.3 0.0 copy-start.5
  4.3 0.7 copy-done.5
  4.9 0.0 copy-start.6
  4.9 0.7 copy-done.6
  5.6 77.8 %shard_map.94 = (f32[16,128]{1,0:T(8,128)S(1)}, f32[16,128]{1,0:T(8,128)S(1)}, f32[16,128]{1,0:T(8,128)S(1)}) custom-call(f32[16,128]{1,0:T(8,128)S(1)} %copy-done.1, f32[16]{0:T(128)S(1)} %copy-done.5, f32[2]{0:T(128)S(1)} %copy-done.6, f32[128,128]{1,0:T(8,128)S(1)} %copy-done, f32[16,128]{1,0:T(8,128)S(1)} %copy-done.2, f32[16,128]{1,0:T(8,128)S(1)} %copy-done.3, ...), custom_call_target="tpu_custom_call" | custom-call | tf_op jit(solution)/shard_map/pallas_call | solution.py:482
  83.4 0.6 copy.13
  84.0 0.6 copy.14
  84.6 0.6 copy.15
Async XLA Ops:
  0.6 0.8 copy-start
  1.5 0.7 copy-start.1
  2.2 0.7 copy-start.2
  2.9 0.7 copy-start.3
  3.6 0.7 copy-start.4
  4.3 0.7 copy-start.5
  4.9 0.7 copy-start.6

commit v2 on v1

--- a/solution.py
+++ b/solution.py
@@ -70,22 +70,25 @@
 
 
 def kernel(
+    points_hbm, ls_hbm, var_hbm, factor_hbm, solution_hbm, residual_hbm, direction_hbm,
+    sol_out, res_out, dir_out,
     points_ref, ls_ref, var_ref, factor_ref, solution_ref, residual_ref, direction_ref,
-    sol_out, res_out, dir_out,
     item, items, zitems, a_mat, dp, bt, dq, btf, dqf,
     t_a, t_b, h_a, h_b, l_a, l_b, ft_a, ft_b, fh_a, fh_b, fl_a, fl_b,
     left, right, right_f, lsend, lrx, rsend, rrx,
-    g_send, g_rx, g_piece, g_px, g_tot, g_all, core_ref,
-    v_send, v_rx, v_piece, v_px, v_tot, v_all, projres_ref,
-    send_sem, recv_sem,
+    g_send, g_rx, g_piece, g_zx, g_tot, g_all, core_ref,
+    v_give, v_take, v_chip, v_px, v_plane, v_zx, v_mine, v_all,
+    in_sem, send_sem, recv_sem, item_sem,
 ):
     nz, npl = Z_HI * Z_LO, X * Y * 2
     tp = npl // 2
     pairs, half_shift, single = shifts_of(nz)
-    probes = direction_ref.shape[0]
+    probes = direction_hbm.shape[0]
+    half_np = npl // 2
     row, col = lax.axis_index("row"), lax.axis_index("col")
     z = rem(div(col, 2), Z_HI) * Z_LO + div(row, Y)
-    s = (div(col, 2 * Z_HI) * Y + rem(row, Y)) * 2 + rem(col, 2)
+    core = rem(col, 2)
+    s = (div(col, 2 * Z_HI) * Y + rem(row, Y)) * 2 + core
 
     def device(zz, ss):
         r = rem(zz, Z_LO) * Y + rem(div(ss, 2), Y)
@@ -94,6 +97,9 @@
 
     def in_plane(j):
         return device(z, rem(s + j + npl, npl))
+
+    def other_core():
+        return device(z, s + 1 - 2 * core)
 
     def in_column(i):
         return device(rem(z + i + nz, nz), s)
@@ -117,6 +123,18 @@
     barrier = pltpu.get_barrier_semaphore()
     loop(1, npl, lambda j: pl.semaphore_signal(barrier, inc=1, device_id=in_plane(j), device_id_type=MESH))
     loop(1, nz, lambda i: pl.semaphore_signal(barrier, inc=1, device_id=in_column(i), device_id_type=MESH))
+
+    loads = [
+        pltpu.make_async_copy(src, dst, in_sem.at[i])
+        for i, (src, dst) in enumerate((
+            (ls_hbm, ls_ref), (var_hbm, var_ref), (points_hbm, points_ref), (direction_hbm, direction_ref),
+            (factor_hbm, factor_ref), (residual_hbm, residual_ref), (solution_hbm, solution_ref),
+        ))
+    ]
+    for load in loads:
+        load.start()
+    for load in loads:
+        load.wait()
 
     sub16 = lax.broadcasted_iota(jnp.int32, (16, 128), 0)
     lane16 = lax.broadcasted_iota(jnp.int32, (16, 128), 1)
@@ -130,22 +148,40 @@
     item[16:32, :] = direction
     pl.semaphore_wait(barrier, npl + nz - 2)
 
-    loop(1, npl, lambda j: send(0, item, items.at[j], in_plane(j)))
+    def give(src, position, target):
+        pltpu.make_async_remote_copy(
+            src_ref=src, dst_ref=items.at[position], send_sem=send_sem.at[0], recv_sem=item_sem.at[position],
+            device_id=target, device_id_type=MESH,
+        ).start()
+
+    def at_other_core(position):
+        return half_np + rem(position + (half_np - 1) * core, half_np)
+
     shifts = [d for p in pairs for d in p] + [half_shift, single]
     slot_of = {d: i for i, d in enumerate(shifts)}
-    z_order = sorted(shifts, key=lambda d: (d not in pairs[0] if pairs else False, abs(d)))
+    z_order = sorted(shifts, key=lambda d: (d not in pairs[0] if pairs else False, -abs(d)))
     for d in z_order:
         i = slot_of[d]
         pltpu.make_async_remote_copy(
-            src_ref=item, dst_ref=zitems.at[i], send_sem=send_sem.at[1], recv_sem=recv_sem.at[10 + i],
+            src_ref=item, dst_ref=zitems.at[i], send_sem=send_sem.at[1], recv_sem=recv_sem.at[11 + i],
             device_id=in_column(-d), device_id_type=MESH,
         ).start()
+    give(item, at_other_core(0), other_core())
+    loop(1, half_np, lambda m: give(item, m, in_plane(2 * m)))
 
     factor = factor_ref[...]
     gram = lax.dot_general(factor, factor, NT, precision=highest, preferred_element_type=F32)
-    g_send[...] = gram.reshape(g_send.shape)
-    projres_ref[...] = lax.dot_general(residual, factor, NT, precision=highest, preferred_element_type=F32)
-    loop(1, nz, lambda i: send(2, g_send.at[rem(z + i, nz)], g_rx.at[i], in_column(i)))
+    g_rows, per = 128 // npl, max(probes // npl, 1)
+    proj = lax.dot_general(residual, factor, NT, precision=highest, preferred_element_type=F32)
+    g_pad = g_send.shape[1] - g_rows - per
+    for i in range(npl):
+        g_send[i, 0:g_rows, :] = gram[i * g_rows : i * g_rows + g_rows]
+        if i * per < probes:
+            g_send[i, g_rows : g_rows + per, :] = proj[i * per : i * per + per]
+        else:
+            g_send[i, g_rows : g_rows + per, :] = jnp.zeros((per, 128), F32)
+        g_send[i, g_rows + per :, :] = jnp.zeros((g_pad, 128), F32)
+    loop(1, npl, lambda j: send(2, g_send.at[rem(s + j, npl)], g_rx.at[j], in_plane(j)))
 
     def pieces(item_val):
         u, d = item_val[0:16], item_val[16:32]
@@ -185,7 +221,7 @@
 
     def take_z(d, store):
         i = slot_of[d]
-        wait(recv_sem, 10 + i, zitems.at[i])
+        wait(recv_sem, 11 + i, zitems.at[i])
         store(build_b(zitems[i]))
 
     def into(qt, half):
@@ -199,12 +235,29 @@
         btf[...] = bd[0]
         dqf[...] = bd[1]
 
-    wait(recv_sem, 0, items.at[pl.ds(1, npl - 1)])
-    loop(1, npl, lambda j: build_a(j, items[j]))
+    def prepare(k):
+        for i in range(2):
+            position = 2 * k + i
+            if isinstance(position, int) and position == 0:
+                continue
+            here = items.at[position]
+            pltpu.make_async_copy(here, here, item_sem.at[position]).wait()
+            yield position
+
+    def prepare_even(k):
+        for position in prepare(k):
+            give(items.at[position], at_other_core(position), other_core())
+            build_a(position, items[position])
+
+    def prepare_odd(k):
+        for position in prepare(k):
+            build_a(position, items[position])
 
     def place(k):
         kk = k + (tp // 2) * div(k + 64 - 3 * tp // 2, 64)
-        return div(kk, tp), rem(kk, tp)
+        qt, r = div(kk, tp), rem(kk, tp)
+        is_half = div(qt + 2, 3) * div(4 - qt, 3)
+        return qt, r + is_half * (tp // 4) * div(r, tp // 4)
 
     bufs = ((t_a, h_a, l_a), (t_b, h_b, l_b))
 
@@ -225,19 +278,22 @@
         left[qt, :, at] = dot(d_q, hi) + dot(d_q, lo)
         right[qt] += dot_nt(d_p, hi) + dot_nt(d_p, lo)
 
-    def steps(first, last):
+    def steps(first, last, prepared=None):
         def one(k, par):
+            if prepared:
+                prepared(k)
             apply(k - 2, par)
             elementwise(1 - par)
             cross(k, par)
 
         k = first
         if first == 0:
+            prepared(0)
             cross(0, 0)
+            prepared(1)
             elementwise(0)
-            if last > 1:
-                cross(1, 1)
-            k = min(2, last)
+            cross(1, 1)
+            k = 2
         if (last - k) % 2 == 0 and last - k >= 4:
 
             def two(i):
@@ -258,24 +314,25 @@
 
     def gram_stage(stage):
         if stage == 0:
-            wait(recv_sem, 2, g_rx.at[pl.ds(1, nz - 1)])
-            total = g_send[z]
+            wait(recv_sem, 2, g_rx.at[pl.ds(1, npl - 1)])
+            total = g_send[s]
+            for j in range(1, npl):
+                total = total + g_rx[j]
+            g_piece[...] = total
+            loop(1, nz, lambda i: send(4, g_piece, g_zx.at[i], in_column(i)))
+        elif stage == 1:
+            wait(recv_sem, 4, g_zx.at[pl.ds(1, nz - 1)])
+            total = g_piece[...]
             for i in range(1, nz):
-                total = total + g_rx[i]
-            g_piece[...] = total
-            loop(1, npl, lambda j: send(4, g_piece, g_px.at[j], in_plane(j)))
-        elif stage == 1:
-            wait(recv_sem, 4, g_px.at[pl.ds(1, npl - 1)])
-            total = g_piece[...]
-            for j in range(1, npl):
-                total = total + g_px[j]
+                total = total + g_zx[i]
             g_tot[...] = total
-            g_all[z] = total
-            loop(1, nz, lambda i: send(5, g_tot, g_all.at[z], in_column(i)))
+            g_all[s] = total
+            loop(1, npl, lambda j: send(5, g_tot, g_all.at[s], in_plane(j)))
         else:
-            wait(recv_sem, 5, g_rx.at[pl.ds(1, nz - 1)])
+            wait(recv_sem, 5, g_rx.at[pl.ds(1, npl - 1)])
             eye = lax.broadcasted_iota(jnp.int32, (128, 128), 0) == lax.broadcasted_iota(jnp.int32, (128, 128), 1)
-            core_ref[...] = g_all[...].reshape(128, 128) + jnp.where(eye, noise, 0.0)
+            gram = jnp.concatenate([g_all[i, 0:g_rows, :] for i in range(npl)], axis=0)
+            core_ref[...] = gram + jnp.where(eye, noise, 0.0)
 
     lane128 = lax.broadcasted_iota(jnp.int32, (128, 128), 1)
     sub128 = lax.broadcasted_iota(jnp.int32, (128, 128), 0)
@@ -293,17 +350,17 @@
     if pairs:
         take_z(pairs[0][0], into(0, 0))
         take_z(pairs[0][1], into(0, 1))
-    steps(0, tp)
+    steps(0, tp // 2, prepare_even)
+    steps(tp // 2, tp, prepare_odd)
     gram_stage(0)
     take_z(half_shift, into(1, 1))
     steps(tp, tp + tp // 2)
     if pairs:
         send_right(0, ((0, pairs[0][0]), (1, pairs[0][1])))
-    middle = lanes(tp * 128, 128)
+    middle = lanes(npl // 4 * 128, 128)
     hi, lo = split2(matern(dot(bt[1], a_mat[:, middle])))
     d_p = dp[:, middle]
     right[1] += dot_nt(d_p, hi) + dot_nt(d_p, lo)
-    gram_stage(1)
     end = tp + tp // 2
     for n, pair in enumerate(pairs[1:]):
         take_z(pair[0], into(2 + n, 0))
@@ -322,7 +379,7 @@
         send_right(len(pairs), ((0, pairs[-1][0]), (1, pairs[-1][1])))
     else:
         send_right(1, ((1, half_shift),))
-    gram_stage(2)
+    gram_stage(1)
 
     fbufs = ((ft_a, fh_a, fl_a), (ft_b, fh_b, fl_b))
 
@@ -349,7 +406,8 @@
                     total = total + (left[qt, 0:16, at] + left[qt, 16:32, at])
             lsend[j] = total
             if not mine:
-                send(6, lsend.at[j], lrx.at[npl - j], in_plane(-j))
+                slot = 2 * rem(j, half_np) + div(j, half_np)
+                send(6, lsend.at[j], lrx.at[npl - slot], in_plane(-slot))
 
     count = npl // 4
 
@@ -374,8 +432,6 @@
     i = slot_of[single]
     rsend[i] = right_f[0:16, :] + right_f[16:32, :]
     send(3, rsend.at[i], rrx.at[i], in_column(single))
-
-    loop(0, 64, sweep)
 
     wait(recv_sem, 6, lrx.at[pl.ds(1, npl - 1)])
     wait(recv_sem, 3, rrx)
@@ -387,45 +443,54 @@
     image = (var_ref[0] * POLY) * total + noise * direction
 
     proj_im = lax.dot_general(image, factor, NT, precision=highest, preferred_element_type=F32)
-    proj_re = projres_ref[...]
+    products = ((direction, image), (residual, image), (image, image), (residual, residual))
     scalars = jnp.zeros((16, 128), F32)
-    for n, (a, b) in enumerate(((direction, image), (residual, image), (image, image), (residual, residual))):
-        scalars = jnp.where(lane16 == n, jnp.sum(a * b, axis=1, keepdims=True), scalars)
-    per = probes // nz
+    for n, (a, b) in enumerate(products):
+        scalars = jnp.where(lane16 == rem(sub16, 8) * 4 + n, jnp.sum(a * b, axis=1, keepdims=True), scalars)
+
+    def half_of(c):
+        first = c == 0
+        rows = jnp.where(first, proj_im[0:8], proj_im[8:16])
+        inner = jnp.where(first, scalars[0:8], scalars[8:16])
+        return rows, jnp.sum(inner, axis=0, keepdims=True)
+
+    for ref, (rows, inner) in ((v_give, half_of(1 - core)), (v_chip, half_of(core))):
+        for p in range(8):
+            ref[p] = rows[p : p + 1]
+        ref[8] = inner
+    send(7, v_give, v_take, other_core())
+    wait(recv_sem, 7, v_take)
+    v_chip[...] += v_take[...]
+    loop(1, half_np, lambda m: send(8, v_chip, v_px.at[m], in_plane(2 * m)))
+    gram_stage(2)
+    loop(0, 44, sweep)
+    wait(recv_sem, 8, v_px.at[pl.ds(1, half_np - 1)])
+    total = v_chip[...]
+    for m in range(1, half_np):
+        total = total + v_px[m]
+    v_plane[...] = total
+    loop(1, nz, lambda i: send(9, v_plane, v_zx.at[i], in_column(i)))
+    loop(44, 128, sweep)
+    wait(recv_sem, 9, v_zx.at[pl.ds(1, nz - 1)])
+    total = v_plane[...]
+    for i in range(1, nz):
+        total = total + v_zx[i]
+    v_mine[...] = total
+    v_all[core] = total
+    send(10, v_mine, v_all.at[core], other_core())
+    core_inv = -core_ref[...]
+    proj_re = jnp.zeros((16, 128), F32)
     for p in range(probes):
-        for n, v in enumerate((proj_im, proj_re, scalars)):
-            at = (p % per) * 4 + n
-            v_send[p // per, at : at + 1, :] = v[p : p + 1, :]
-        at = (p % per) * 4 + 3
-        v_send[p // per, at : at + 1, :] = jnp.zeros((1, 128), F32)
-    loop(1, nz, lambda i: send(7, v_send.at[rem(z + i, nz)], v_rx.at[i], in_column(i)))
-    loop(64, 96, sweep)
-    wait(recv_sem, 7, v_rx.at[pl.ds(1, nz - 1)])
-    total = v_send[z]
-    for i in range(1, nz):
-        total = total + v_rx[i]
-    v_piece[...] = total
-    loop(1, npl, lambda j: send(8, v_piece, v_px.at[j], in_plane(j)))
-    loop(96, 128, sweep)
-    wait(recv_sem, 8, v_px.at[pl.ds(1, npl - 1)])
-    total = v_piece[...]
-    for j in range(1, npl):
-        total = total + v_px[j]
-    v_tot[...] = total
-    v_all[z] = total
-    loop(1, nz, lambda i: send(9, v_tot, v_all.at[z], in_column(i)))
-    core_inv = -core_ref[...]
-    wait(recv_sem, 9, v_rx.at[pl.ds(1, nz - 1)])
-
-    def gathered(n):
-        out = jnp.zeros((16, 128), F32)
-        for p in range(probes):
-            at = (p % per) * 4 + n
-            out = jnp.where(sub16 == p, v_all[p // per, at : at + 1, :], out)
-        return out
-
-    proj_im, proj_re, scalars = gathered(0), gathered(1), gathered(2)
-    d_im, r_im, im_im, r_r = (scalars[:, n : n + 1] for n in range(4))
+        at = g_rows + p % per
+        proj_re = jnp.where(sub16 == p, g_all[p // per, at : at + 1, :], proj_re)
+    wait(recv_sem, 10, v_take)
+    proj_im = jnp.zeros((16, 128), F32)
+    for p in range(probes):
+        proj_im = jnp.where(sub16 == p, v_all[p // 8, p % 8], proj_im)
+    inner = jnp.where(sub16 < 8, v_all[0, 8], v_all[1, 8])
+    d_im, r_im, im_im, r_r = (
+        jnp.sum(jnp.where(lane16 == rem(sub16, 8) * 4 + n, inner, 0.0), axis=1, keepdims=True) for n in range(4)
+    )
     both = jnp.dot(
         jnp.concatenate([proj_re, proj_im], axis=0), core_inv, precision=highest, preferred_element_type=F32
     )
@@ -445,14 +510,20 @@
 
     wait(send_sem, 0, items.at[pl.ds(1, npl - 1)])
     wait(send_sem, 1, zitems)
-    wait(send_sem, 2, g_rx.at[pl.ds(1, nz - 1)])
+    wait(send_sem, 2, g_rx.at[pl.ds(1, npl - 1)])
     wait(send_sem, 3, rrx)
-    wait(send_sem, 4, g_px.at[pl.ds(1, npl - 1)])
-    wait(send_sem, 5, g_rx.at[pl.ds(1, nz - 1)])
+    wait(send_sem, 4, g_zx.at[pl.ds(1, nz - 1)])
+    wait(send_sem, 5, g_rx.at[pl.ds(1, npl - 1)])
     wait(send_sem, 6, lrx.at[pl.ds(1, npl - 1)])
-    wait(send_sem, 7, v_rx.at[pl.ds(1, nz - 1)])
-    wait(send_sem, 8, v_px.at[pl.ds(1, npl - 1)])
-    wait(send_sem, 9, v_rx.at[pl.ds(1, nz - 1)])
+    wait(send_sem, 7, v_take)
+    wait(send_sem, 8, v_px.at[pl.ds(1, half_np - 1)])
+    wait(send_sem, 9, v_zx.at[pl.ds(1, nz - 1)])
+    wait(send_sem, 10, v_take)
+
+
+def hand_out(*refs):
+    for src, dst in zip(refs[:3], refs[3:]):
+        dst[...] = src[...]
 
 
 def local(points, lengthscales, variances, factor, solution, residual, direction):
@@ -460,10 +531,11 @@
     pairs, _, _ = shifts_of(nz)
     blocks = 2 * len(pairs) + 2
     nq = 2 + max(len(pairs) - 1, 0)
-    gr, vr = 128 // nz, 4 * (16 // nz)
+    gr, vr = -(-(128 // npl + max(16 // npl, 1)) // 8) * 8, (9, 1, 128)
     wide = (npl + 1) * 128
     vmem = pl.BlockSpec(memory_space=pltpu.VMEM)
-    smem = pl.BlockSpec(memory_space=pltpu.SMEM)
+    held = [pltpu.VMEM, pltpu.SMEM, pltpu.SMEM, pltpu.VMEM, pltpu.VMEM, pltpu.VMEM, pltpu.VMEM]
+    args = (points, lengthscales, variances, factor, solution, residual, direction)
     tile, ftile = (256, 256), (128, 512)
     scratch = [
         ((32, 128), F32), ((npl, 32, 128), F32), ((blocks, 32, 128), F32),
@@ -473,23 +545,29 @@
         (ftile, F32), (ftile, F32), (ftile, BF16), (ftile, BF16), (ftile, BF16), (ftile, BF16),
         ((nq, 32, npl * 128), F32), ((nq, 32, 256), F32), ((32, 128), F32),
         ((npl + 1, 16, 128), F32), ((npl, 16, 128), F32), ((blocks, 16, 128), F32), ((blocks, 16, 128), F32),
-        ((nz, gr, 128), F32), ((nz, gr, 128), F32), ((gr, 128), F32), ((npl, gr, 128), F32),
-        ((gr, 128), F32), ((nz, gr, 128), F32), ((128, 128), F32),
-        ((nz, vr, 128), F32), ((nz, vr, 128), F32), ((vr, 128), F32), ((npl, vr, 128), F32),
-        ((vr, 128), F32), ((nz, vr, 128), F32), ((16, 128), F32),
+        ((npl, gr, 128), F32), ((npl, gr, 128), F32), ((gr, 128), F32), ((nz, gr, 128), F32),
+        ((gr, 128), F32), ((npl, gr, 128), F32), ((128, 128), F32),
+        (vr, F32), (vr, F32), (vr, F32), ((npl // 2, *vr), F32), (vr, F32), ((nz, *vr), F32), (vr, F32), ((2, *vr), F32),
     ]
     out = jax.ShapeDtypeStruct(direction.shape, F32)
-    return pl.pallas_call(
+    outs = pl.pallas_call(
         kernel,
         out_shape=(out, out, out),
-        in_specs=[vmem, smem, smem, vmem, vmem, vmem, vmem],
+        in_specs=[pl.BlockSpec(memory_space=pl.ANY)] * len(args),
         out_specs=(vmem, vmem, vmem),
-        scratch_shapes=[pltpu.VMEM(shape, dtype) for shape, dtype in scratch]
-        + [pltpu.SemaphoreType.DMA((10,)), pltpu.SemaphoreType.DMA((10 + blocks,))],
+        scratch_shapes=[space(a.shape, F32) for space, a in zip(held, args)]
+        + [pltpu.VMEM(shape, dtype) for shape, dtype in scratch]
+        + [pltpu.SemaphoreType.DMA((n,)) for n in (len(args), 11, 11 + blocks, npl)],
         compiler_params=pltpu.CompilerParams(
-            collective_id=0, has_side_effects=True, vmem_limit_bytes=40 * 2**20
+            collective_id=0, has_side_effects=True, vmem_limit_bytes=56 * 2**20
         ),
-    )(points, lengthscales, variances, factor, solution, residual, direction)
+    )(*args)
+    return pl.pallas_call(
+        hand_out,
+        out_shape=(out, out, out),
+        in_specs=[vmem] * 3,
+        out_specs=(vmem, vmem, vmem),
+    )(*outs)
 
 
 def solution(mesh):

time: 85.6 us -> 68.5 us (0.80)
  Pallas kernels: 77.8 us -> 67.6 us
  local copies, waits for them, and re-layouts: 6.72 us -> 0 us
    pallas_call x1 -> x2, Pallas kernels: 77.8 us -> 67.6 us  [the longest x1 66.3 us: local(): pl.pallas_call(kernel, out_shape=(out, out, out), in_specs=[pl.BlockSpec(...]
    unnamed x17 -> x0, local copies, waits for them, and re-layouts: 6.72 us -> none
where the time goes in v2:
time: 68.5 us; the launch traced here: 68.3 us
  Pallas kernels  67.6 us (99%)
    pallas_call x1, Pallas kernels, local(): pl.pallas_call(kernel, out_shape=(out, out, out), in_specs=[pl.BlockSpec(...  66.3 us

profile of v2, /device:TPU:1, one launch (start us, length us, event | category | flops | bytes accessed | tf_op | source)
XLA Modules:
  0.0 68.3 jit_solution(8701249542401340943)
XLA Ops:
  0.6 66.3 %shard_map.94 = (f32[16,128]{1,0:T(8,128)}, f32[16,128]{1,0:T(8,128)}, f32[16,128]{1,0:T(8,128)}) custom-call(f32[16,128]{1,0:T(8,128)} %points_hbm.1, f32[16]{0:T(128)} %ls_hbm.1, f32[2]{0:T(128)} %var_hbm.1, f32[128,128]{1,0:T(8,128)} %factor_hbm.1, f32[16,128]{1,0:T(8,128)} %solution_hbm.1, f32[16,128]{1,0:T(8,128)} %residual_hbm.1, f32[16,128]{1,0:T(8,128)} %direction_hbm.1), custom_call_target="tpu_custom_call" | custom-call | tf_op jit(solution)/shard_map/pallas_call | solution.py:553
  66.9 1.3 %shard_map.95 = (f32[16,128]{1,0:T(8,128)}, f32[16,128]{1,0:T(8,128)}, f32[16,128]{1,0:T(8,128)}) custom-call(f32[16,128]{1,0:T(8,128)} %get-tuple-element.6.refs_0_, f32[16,128]{1,0:T(8,128)} %get-tuple-element.7.refs_1_, f32[16,128]{1,0:T(8,128)} %get-tuple-element.8.refs_2_), custom_call_target="tpu_custom_call" | custom-call | tf_op jit(solution)/shard_map/pallas_call | solution.py:565

commit v3 on v2

--- a/solution.py
+++ b/solution.py
@@ -61,28 +61,24 @@
     return lax.dot_general(a, b, NT, preferred_element_type=F32)
 
 
-def shifts_of(nz):
-    full = [d if d % 2 else -d for d in range(2, nz // 2)]
-    pairs = [(full[i], full[i + 1]) for i in range(0, len(full), 2)]
-    if len(pairs) > 1:
-        pairs = [pairs[0]] + pairs[:0:-1]
-    return pairs, nz // 2, 1
+PLANES = {16: (((2, 3), (-6, -7), (-5, 4)), -8, 1), 8: (((2, -3),), -4, 1)}
 
 
 def kernel(
     points_hbm, ls_hbm, var_hbm, factor_hbm, solution_hbm, residual_hbm, direction_hbm,
     sol_out, res_out, dir_out,
     points_ref, ls_ref, var_ref, factor_ref, solution_ref, residual_ref, direction_ref,
-    item, items, zitems, a_mat, dp, bt, dq, btf, dqf,
+    item, items, zitems, hub_item, a_mat, dp, bt, dq, btf, dqf,
     t_a, t_b, h_a, h_b, l_a, l_b, ft_a, ft_b, fh_a, fh_b, fl_a, fl_b,
-    left, right, right_f, lsend, lrx, rsend, rrx,
-    g_send, g_rx, g_piece, g_zx, g_tot, g_all, core_ref,
-    v_give, v_take, v_chip, v_px, v_plane, v_zx, v_mine, v_all,
+    left, right, right_f, lsend, lrx, rsend, rrx, hub_rx, hub_out, hub_in,
+    g_send, g_rx, g_piece, g_zx, g_window, g_zy, g_tot, g_all, core_ref,
+    v_give, v_take, v_chip, v_px, v_plane, v_zx, v_window, v_zy, v_mine, v_all,
     in_sem, send_sem, recv_sem, item_sem,
 ):
     nz, npl = Z_HI * Z_LO, X * Y * 2
     tp = npl // 2
-    pairs, half_shift, single = shifts_of(nz)
+    pairs, half_shift, single = PLANES[nz]
+    quarter = nz // 4
     probes = direction_hbm.shape[0]
     half_np = npl // 2
     row, col = lax.axis_index("row"), lax.axis_index("col")
@@ -122,7 +118,14 @@
 
     barrier = pltpu.get_barrier_semaphore()
     loop(1, npl, lambda j: pl.semaphore_signal(barrier, inc=1, device_id=in_plane(j), device_id_type=MESH))
-    loop(1, nz, lambda i: pl.semaphore_signal(barrier, inc=1, device_id=in_column(i), device_id_type=MESH))
+    for sign in (1, -1):
+        loop(
+            1,
+            quarter + 1,
+            lambda i, sign=sign: pl.semaphore_signal(
+                barrier, inc=1, device_id=in_column(sign * i), device_id_type=MESH
+            ),
+        )
 
     loads = [
         pltpu.make_async_copy(src, dst, in_sem.at[i])
@@ -146,7 +149,7 @@
     noise = var_ref[1]
     item[0:16, :] = (points_ref[...] - 0.5) / scale * SCALE
     item[16:32, :] = direction
-    pl.semaphore_wait(barrier, npl + nz - 2)
+    pl.semaphore_wait(barrier, npl - 1 + 2 * quarter)
 
     def give(src, position, target):
         pltpu.make_async_remote_copy(
@@ -159,13 +162,17 @@
 
     shifts = [d for p in pairs for d in p] + [half_shift, single]
     slot_of = {d: i for i, d in enumerate(shifts)}
-    z_order = sorted(shifts, key=lambda d: (d not in pairs[0] if pairs else False, -abs(d)))
-    for d in z_order:
+
+    def give_z(src, d, target):
         i = slot_of[d]
         pltpu.make_async_remote_copy(
-            src_ref=item, dst_ref=zitems.at[i], send_sem=send_sem.at[1], recv_sem=recv_sem.at[11 + i],
-            device_id=in_column(-d), device_id_type=MESH,
+            src_ref=src, dst_ref=zitems.at[i], send_sem=send_sem.at[1], recv_sem=recv_sem.at[16 + i],
+            device_id=target, device_id_type=MESH,
         ).start()
+
+    send(15, item, hub_item, in_column(quarter))
+    for d in sorted((d for d in shifts if d > 0), key=lambda d: d not in pairs[0]):
+        give_z(item, d, in_column(-d))
     give(item, at_other_core(0), other_core())
     loop(1, half_np, lambda m: give(item, m, in_plane(2 * m)))
 
@@ -221,7 +228,7 @@
 
     def take_z(d, store):
         i = slot_of[d]
-        wait(recv_sem, 11 + i, zitems.at[i])
+        wait(recv_sem, 16 + i, zitems.at[i])
         store(build_b(zitems[i]))
 
     def into(qt, half):
@@ -294,13 +301,13 @@
             elementwise(0)
             cross(1, 1)
             k = 2
-        if (last - k) % 2 == 0 and last - k >= 4:
-
-            def two(i):
-                one(2 * i, 0)
-                one(2 * i + 1, 1)
-
-            loop(k // 2, last // 2, two)
+        if k % 8 == 0 and (last - k) % 8 == 0:
+
+            def eight(i):
+                for n in range(8):
+                    one(8 * i + n, n % 2)
+
+            loop(k // 8, last // 8, eight)
         else:
             for kk in range(k, last):
                 one(kk, kk % 2)
@@ -310,7 +317,25 @@
         for h, d in halves:
             i = slot_of[d]
             rsend[i] = both[:, h * 128 : h * 128 + 128]
-            send(3, rsend.at[i], rrx.at[i], in_column(d))
+            if d > 0:
+                send(3, rsend.at[i], rrx.at[d - 1], in_column(d))
+            else:
+                send(11, rsend.at[i], hub_rx.at[-d - quarter - 1], in_column(d + quarter))
+
+    def window(kind, src, rx):
+        loop(1, quarter + 1, lambda i: send(kind, src, rx.at[i - 1], in_column(i)))
+        loop(1, quarter, lambda i: send(kind, src, rx.at[quarter - 1 + i], in_column(-i)))
+
+    def window_sum(kind, own, rx):
+        wait(recv_sem, kind, rx)
+        total = own
+        for i in range(2 * quarter - 1):
+            total = total + rx[i]
+        return total
+
+    def both_windows(kind, src, rx):
+        send(kind, src, rx.at[0], in_column(quarter))
+        send(kind, src, rx.at[1], in_column(-quarter))
 
     def gram_stage(stage):
         if stage == 0:
@@ -319,12 +344,13 @@
             for j in range(1, npl):
                 total = total + g_rx[j]
             g_piece[...] = total
-            loop(1, nz, lambda i: send(4, g_piece, g_zx.at[i], in_column(i)))
+            window(4, g_piece, g_zx)
         elif stage == 1:
-            wait(recv_sem, 4, g_zx.at[pl.ds(1, nz - 1)])
-            total = g_piece[...]
-            for i in range(1, nz):
-                total = total + g_zx[i]
+            g_window[...] = window_sum(4, g_piece[...], g_zx)
+            both_windows(13, g_window, g_zy)
+        elif stage == 2:
+            wait(recv_sem, 13, g_zy)
+            total = g_zy[0] + g_zy[1]
             g_tot[...] = total
             g_all[s] = total
             loop(1, npl, lambda j: send(5, g_tot, g_all.at[s], in_plane(j)))
@@ -347,30 +373,36 @@
         new = jnp.where(sub128 == k, line, m - column * line)
         core_ref[...] = jnp.where(lane128 == k, jnp.where(sub128 == k, -inv, column * inv), new)
 
-    if pairs:
-        take_z(pairs[0][0], into(0, 0))
+    take_z(pairs[0][0], into(0, 0))
+    if pairs[0][1] > 0:
+        take_z(pairs[0][1], into(0, 1))
+    wait(recv_sem, 15, hub_item)
+    for d in sorted((d for d in shifts if d < 0), key=lambda d: (d not in pairs[0], d)):
+        give_z(hub_item, d, in_column(-d - quarter))
+    if pairs[0][1] < 0:
         take_z(pairs[0][1], into(0, 1))
     steps(0, tp // 2, prepare_even)
+    gram_stage(0)
     steps(tp // 2, tp, prepare_odd)
-    gram_stage(0)
     take_z(half_shift, into(1, 1))
-    steps(tp, tp + tp // 2)
-    if pairs:
-        send_right(0, ((0, pairs[0][0]), (1, pairs[0][1])))
+    end = tp + tp // 2
+    steps(tp, end)
+    send_right(0, ((0, pairs[0][0]), (1, pairs[0][1])))
     middle = lanes(npl // 4 * 128, 128)
     hi, lo = split2(matern(dot(bt[1], a_mat[:, middle])))
     d_p = dp[:, middle]
     right[1] += dot_nt(d_p, hi) + dot_nt(d_p, lo)
-    end = tp + tp // 2
     for n, pair in enumerate(pairs[1:]):
         take_z(pair[0], into(2 + n, 0))
         take_z(pair[1], into(2 + n, 1))
-        steps(end, end + tp)
-        end += tp
+        steps(end, end + tp // 2)
         if n == 0:
             send_right(1, ((1, half_shift),))
         else:
             send_right(1 + n, ((0, pairs[n][0]), (1, pairs[n][1])))
+        gram_stage(1 + n)
+        steps(end + tp // 2, end + tp)
+        end += tp
     take_z(single, into_f)
     elementwise((end - 1) % 2)
     apply(end - 2, end % 2)
@@ -379,7 +411,8 @@
         send_right(len(pairs), ((0, pairs[-1][0]), (1, pairs[-1][1])))
     else:
         send_right(1, ((1, half_shift),))
-    gram_stage(1)
+        gram_stage(1)
+        gram_stage(2)
 
     fbufs = ((ft_a, fh_a, fl_a), (ft_b, fh_b, fl_b))
 
@@ -431,15 +464,25 @@
     f_apply(count - 1, (count - 1) % 2, last=True)
     i = slot_of[single]
     rsend[i] = right_f[0:16, :] + right_f[16:32, :]
-    send(3, rsend.at[i], rrx.at[i], in_column(single))
+    send(3, rsend.at[i], rrx.at[single - 1], in_column(single))
+    wait(recv_sem, 11, hub_rx)
+    total = hub_rx[0]
+    for i in range(1, quarter):
+        total = total + hub_rx[i]
+    hub_out[...] = total
+    send(12, hub_out, hub_in, in_column(-quarter))
+    gram_stage(3)
+    loop(0, 16, sweep)
 
     wait(recv_sem, 6, lrx.at[pl.ds(1, npl - 1)])
     wait(recv_sem, 3, rrx)
     total = lsend[npl] + (right[1, 0:16, 0:128] + right[1, 16:32, 0:128])
     for j in range(1, npl):
         total = total + lrx[j]
-    for i in range(len(shifts)):
+    for i in range(quarter):
         total = total + rrx[i]
+    wait(recv_sem, 12, hub_in)
+    total = total + hub_in[...]
     image = (var_ref[0] * POLY) * total + noise * direction
 
     proj_im = lax.dot_general(image, factor, NT, precision=highest, preferred_element_type=F32)
@@ -462,19 +505,19 @@
     wait(recv_sem, 7, v_take)
     v_chip[...] += v_take[...]
     loop(1, half_np, lambda m: send(8, v_chip, v_px.at[m], in_plane(2 * m)))
-    gram_stage(2)
-    loop(0, 44, sweep)
+    loop(16, 60, sweep)
     wait(recv_sem, 8, v_px.at[pl.ds(1, half_np - 1)])
     total = v_chip[...]
     for m in range(1, half_np):
         total = total + v_px[m]
     v_plane[...] = total
-    loop(1, nz, lambda i: send(9, v_plane, v_zx.at[i], in_column(i)))
-    loop(44, 128, sweep)
-    wait(recv_sem, 9, v_zx.at[pl.ds(1, nz - 1)])
-    total = v_plane[...]
-    for i in range(1, nz):
-        total = total + v_zx[i]
+    window(9, v_plane, v_zx)
+    loop(60, 96, sweep)
+    v_window[...] = window_sum(9, v_plane[...], v_zx)
+    both_windows(14, v_window, v_zy)
+    loop(96, 128, sweep)
+    wait(recv_sem, 14, v_zy)
+    total = v_zy[0] + v_zy[1]
     v_mine[...] = total
     v_all[core] = total
     send(10, v_mine, v_all.at[core], other_core())
@@ -512,13 +555,18 @@
     wait(send_sem, 1, zitems)
     wait(send_sem, 2, g_rx.at[pl.ds(1, npl - 1)])
     wait(send_sem, 3, rrx)
-    wait(send_sem, 4, g_zx.at[pl.ds(1, nz - 1)])
+    wait(send_sem, 4, g_zx)
     wait(send_sem, 5, g_rx.at[pl.ds(1, npl - 1)])
     wait(send_sem, 6, lrx.at[pl.ds(1, npl - 1)])
     wait(send_sem, 7, v_take)
     wait(send_sem, 8, v_px.at[pl.ds(1, half_np - 1)])
-    wait(send_sem, 9, v_zx.at[pl.ds(1, nz - 1)])
+    wait(send_sem, 9, v_zx)
     wait(send_sem, 10, v_take)
+    wait(send_sem, 11, hub_rx)
+    wait(send_sem, 12, hub_in)
+    wait(send_sem, 13, g_zy)
+    wait(send_sem, 14, v_zy)
+    wait(send_sem, 15, hub_item)
 
 
 def hand_out(*refs):
@@ -528,9 +576,8 @@
 
 def local(points, lengthscales, variances, factor, solution, residual, direction):
     nz, npl = Z_HI * Z_LO, X * Y * 2
-    pairs, _, _ = shifts_of(nz)
-    blocks = 2 * len(pairs) + 2
-    nq = 2 + max(len(pairs) - 1, 0)
+    quarter = nz // 4
+    blocks, nq = 2 * quarter, quarter
     gr, vr = -(-(128 // npl + max(16 // npl, 1)) // 8) * 8, (9, 1, 128)
     wide = (npl + 1) * 128
     vmem = pl.BlockSpec(memory_space=pltpu.VMEM)
@@ -538,16 +585,19 @@
     args = (points, lengthscales, variances, factor, solution, residual, direction)
     tile, ftile = (256, 256), (128, 512)
     scratch = [
-        ((32, 128), F32), ((npl, 32, 128), F32), ((blocks, 32, 128), F32),
+        ((32, 128), F32), ((npl, 32, 128), F32), ((blocks, 32, 128), F32), ((32, 128), F32),
         ((128, wide), BF16), ((32, wide), BF16), ((nq, 256, 128), BF16), ((nq, 32, 256), BF16),
         ((128, 128), BF16), ((32, 128), BF16),
         (tile, F32), (tile, F32), (tile, BF16), (tile, BF16), (tile, BF16), (tile, BF16),
         (ftile, F32), (ftile, F32), (ftile, BF16), (ftile, BF16), (ftile, BF16), (ftile, BF16),
         ((nq, 32, npl * 128), F32), ((nq, 32, 256), F32), ((32, 128), F32),
-        ((npl + 1, 16, 128), F32), ((npl, 16, 128), F32), ((blocks, 16, 128), F32), ((blocks, 16, 128), F32),
-        ((npl, gr, 128), F32), ((npl, gr, 128), F32), ((gr, 128), F32), ((nz, gr, 128), F32),
+        ((npl + 1, 16, 128), F32), ((npl, 16, 128), F32), ((blocks, 16, 128), F32), ((quarter, 16, 128), F32),
+        ((quarter, 16, 128), F32), ((16, 128), F32), ((16, 128), F32),
+        ((npl, gr, 128), F32), ((npl, gr, 128), F32), ((gr, 128), F32), ((blocks - 1, gr, 128), F32),
+        ((gr, 128), F32), ((2, gr, 128), F32),
         ((gr, 128), F32), ((npl, gr, 128), F32), ((128, 128), F32),
-        (vr, F32), (vr, F32), (vr, F32), ((npl // 2, *vr), F32), (vr, F32), ((nz, *vr), F32), (vr, F32), ((2, *vr), F32),
+        (vr, F32), (vr, F32), (vr, F32), ((npl // 2, *vr), F32), (vr, F32), ((blocks - 1, *vr), F32), (vr, F32),
+        ((2, *vr), F32), (vr, F32), ((2, *vr), F32),
     ]
     out = jax.ShapeDtypeStruct(direction.shape, F32)
     outs = pl.pallas_call(
@@ -557,7 +607,7 @@
         out_specs=(vmem, vmem, vmem),
         scratch_shapes=[space(a.shape, F32) for space, a in zip(held, args)]
         + [pltpu.VMEM(shape, dtype) for shape, dtype in scratch]
-        + [pltpu.SemaphoreType.DMA((n,)) for n in (len(args), 11, 11 + blocks, npl)],
+        + [pltpu.SemaphoreType.DMA((n,)) for n in (len(args), 16, 16 + blocks, npl)],
         compiler_params=pltpu.CompilerParams(
             collective_id=0, has_side_effects=True, vmem_limit_bytes=56 * 2**20
         ),

time: 68.5 us -> 65.8 us (0.961)
  Pallas kernels: 67.6 us -> 65 us
    pallas_call x1, Pallas kernels: 66.3 us -> 63.6 us  [local(): pl.pallas_call(kernel, out_shape=(out, out, out), in_specs=[pl.BlockSpec(...]
where the time goes in v3:
time: 65.8 us; the launch traced here: 65.6 us
  Pallas kernels  65 us (99%)
    pallas_call x1, Pallas kernels, local(): pl.pallas_call(kernel, out_shape=(out, out, out), in_specs=[pl.BlockSpec(...  63.6 us
    pallas_call x1, Pallas kernels, local(): pl.pallas_call(hand_out, out_shape=(out, out, out), in_specs=[vmem] * 3,...  1.34 us

profile of v3, /device:TPU:1, one launch (start us, length us, event | category | flops | bytes accessed | tf_op | source)
XLA Modules:
  0.0 65.6 jit_solution(4890983208279447949)
XLA Ops:
  0.6 63.6 %shard_map.94 = (f32[16,128]{1,0:T(8,128)}, f32[16,128]{1,0:T(8,128)}, f32[16,128]{1,0:T(8,128)}) custom-call(f32[16,128]{1,0:T(8,128)} %points_hbm.1, f32[16]{0:T(128)} %ls_hbm.1, f32[2]{0:T(128)} %var_hbm.1, f32[128,128]{1,0:T(8,128)} %factor_hbm.1, f32[16,128]{1,0:T(8,128)} %solution_hbm.1, f32[16,128]{1,0:T(8,128)} %residual_hbm.1, f32[16,128]{1,0:T(8,128)} %direction_hbm.1), custom_call_target="tpu_custom_call" | custom-call | tf_op jit(solution)/shard_map/pallas_call | solution.py:603
  64.3 1.3 %shard_map.95 = (f32[16,128]{1,0:T(8,128)}, f32[16,128]{1,0:T(8,128)}, f32[16,128]{1,0:T(8,128)}) custom-call(f32[16,128]{1,0:T(8,128)} %get-tuple-element.6.refs_0_, f32[16,128]{1,0:T(8,128)} %get-tuple-element.7.refs_1_, f32[16,128]{1,0:T(8,128)} %get-tuple-element.8.refs_2_), custom_call_target="tpu_custom_call" | custom-call | tf_op jit(solution)/shard_map/pallas_call | solution.py:615

commit v4 on v3

--- a/solution.py
+++ b/solution.py
@@ -72,7 +72,7 @@
     t_a, t_b, h_a, h_b, l_a, l_b, ft_a, ft_b, fh_a, fh_b, fl_a, fl_b,
     left, right, right_f, lsend, lrx, rsend, rrx, hub_rx, hub_out, hub_in,
     g_send, g_rx, g_piece, g_zx, g_window, g_zy, g_tot, g_all, core_ref,
-    v_give, v_take, v_chip, v_px, v_plane, v_zx, v_window, v_zy, v_mine, v_all,
+    v_give, v_take, v_chip, v_px, v_plane, v_zx, v_window, v_zy, v_all,
     in_sem, send_sem, recv_sem, item_sem,
 ):
     nz, npl = Z_HI * Z_LO, X * Y * 2
@@ -97,8 +97,8 @@
     def other_core():
         return device(z, s + 1 - 2 * core)
 
-    def in_column(i):
-        return device(rem(z + i + nz, nz), s)
+    def in_column(i, other=0):
+        return device(rem(z + i + nz, nz), s + other * (1 - 2 * core))
 
     def send(kind, src, dst, target):
         pltpu.make_async_remote_copy(
@@ -115,17 +115,6 @@
             return carry
 
         lax.fori_loop(lo, hi, step, 0)
-
-    barrier = pltpu.get_barrier_semaphore()
-    loop(1, npl, lambda j: pl.semaphore_signal(barrier, inc=1, device_id=in_plane(j), device_id_type=MESH))
-    for sign in (1, -1):
-        loop(
-            1,
-            quarter + 1,
-            lambda i, sign=sign: pl.semaphore_signal(
-                barrier, inc=1, device_id=in_column(sign * i), device_id_type=MESH
-            ),
-        )
 
     loads = [
         pltpu.make_async_copy(src, dst, in_sem.at[i])
@@ -136,7 +125,20 @@
     ]
     for load in loads:
         load.start()
-    for load in loads:
+    barrier = pltpu.get_barrier_semaphore()
+    loop(1, npl, lambda j: pl.semaphore_signal(barrier, inc=1, device_id=in_plane(j), device_id_type=MESH))
+    for sign in (1, -1):
+        far = in_column(sign * quarter, 1)
+        pl.semaphore_signal(barrier, inc=1, device_id=far, device_id_type=MESH)
+        loop(
+            1,
+            quarter + 1,
+            lambda i, sign=sign: pl.semaphore_signal(
+                barrier, inc=1, device_id=in_column(sign * i), device_id_type=MESH
+            ),
+        )
+
+    for load in loads[:4]:
         load.wait()
 
     sub16 = lax.broadcasted_iota(jnp.int32, (16, 128), 0)
@@ -145,11 +147,10 @@
     for i in range(16):
         scale = jnp.where(sub16 == i, ls_ref[i], scale)
     direction = direction_ref[...]
-    residual = residual_ref[...]
     noise = var_ref[1]
     item[0:16, :] = (points_ref[...] - 0.5) / scale * SCALE
     item[16:32, :] = direction
-    pl.semaphore_wait(barrier, npl - 1 + 2 * quarter)
+    pl.semaphore_wait(barrier, npl - 1 + 2 * quarter + 2)
 
     def give(src, position, target):
         pltpu.make_async_remote_copy(
@@ -176,6 +177,9 @@
     give(item, at_other_core(0), other_core())
     loop(1, half_np, lambda m: give(item, m, in_plane(2 * m)))
 
+    for load in loads[4:]:
+        load.wait()
+    residual = residual_ref[...]
     factor = factor_ref[...]
     gram = lax.dot_general(factor, factor, NT, precision=highest, preferred_element_type=F32)
     g_rows, per = 128 // npl, max(probes // npl, 1)
@@ -514,19 +518,22 @@
     window(9, v_plane, v_zx)
     loop(60, 96, sweep)
     v_window[...] = window_sum(9, v_plane[...], v_zx)
-    both_windows(14, v_window, v_zy)
+    for other in (0, 1):
+        send(14, v_window, v_zy.at[core, 0], in_column(quarter, other))
+        send(14, v_window, v_zy.at[core, 1], in_column(-quarter, other))
     loop(96, 128, sweep)
-    wait(recv_sem, 14, v_zy)
-    total = v_zy[0] + v_zy[1]
-    v_mine[...] = total
-    v_all[core] = total
-    send(10, v_mine, v_all.at[core], other_core())
     core_inv = -core_ref[...]
+    both_inv = jnp.concatenate(
+        [core_inv, jnp.dot(core_inv, factor, precision=highest, preferred_element_type=F32)], axis=1
+    )
     proj_re = jnp.zeros((16, 128), F32)
     for p in range(probes):
         at = g_rows + p % per
         proj_re = jnp.where(sub16 == p, g_all[p // per, at : at + 1, :], proj_re)
-    wait(recv_sem, 10, v_take)
+    of_re = jnp.dot(proj_re, both_inv, precision=highest, preferred_element_type=F32)
+    wait(recv_sem, 14, v_zy)
+    for h in range(2):
+        v_all[h] = v_zy[h, 0] + v_zy[h, 1]
     proj_im = jnp.zeros((16, 128), F32)
     for p in range(probes):
         proj_im = jnp.where(sub16 == p, v_all[p // 8, p % 8], proj_im)
@@ -534,10 +541,8 @@
     d_im, r_im, im_im, r_r = (
         jnp.sum(jnp.where(lane16 == rem(sub16, 8) * 4 + n, inner, 0.0), axis=1, keepdims=True) for n in range(4)
     )
-    both = jnp.dot(
-        jnp.concatenate([proj_re, proj_im], axis=0), core_inv, precision=highest, preferred_element_type=F32
-    )
-    coef_re, coef_im = both[0:16], both[16:32]
+    of_im = jnp.dot(proj_im, both_inv, precision=highest, preferred_element_type=F32)
+    coef_re, coef_im = of_re[:, 0:128], of_im[:, 0:128]
     res_z = (r_r - jnp.sum(proj_re * coef_re, axis=1, keepdims=True)) / noise
     alpha = res_z / d_im
     coef_new = coef_re - alpha * coef_im
@@ -548,7 +553,7 @@
     new_residual = residual - alpha * image
     sol_out[...] = solution_ref[...] + alpha * direction
     res_out[...] = new_residual
-    fitted = jnp.dot(coef_new, factor, precision=highest, preferred_element_type=F32)
+    fitted = of_re[:, 128:256] - alpha * of_im[:, 128:256]
     dir_out[...] = (new_residual - fitted) / noise + beta * direction
 
     wait(send_sem, 0, items.at[pl.ds(1, npl - 1)])
@@ -561,7 +566,6 @@
     wait(send_sem, 7, v_take)
     wait(send_sem, 8, v_px.at[pl.ds(1, half_np - 1)])
     wait(send_sem, 9, v_zx)
-    wait(send_sem, 10, v_take)
     wait(send_sem, 11, hub_rx)
     wait(send_sem, 12, hub_in)
     wait(send_sem, 13, g_zy)
@@ -597,7 +601,7 @@
         ((gr, 128), F32), ((2, gr, 128), F32),
         ((gr, 128), F32), ((npl, gr, 128), F32), ((128, 128), F32),
         (vr, F32), (vr, F32), (vr, F32), ((npl // 2, *vr), F32), (vr, F32), ((blocks - 1, *vr), F32), (vr, F32),
-        ((2, *vr), F32), (vr, F32), ((2, *vr), F32),
+        ((2, 2, *vr), F32), ((2, *vr), F32),
     ]
     out = jax.ShapeDtypeStruct(direction.shape, F32)
     outs = pl.pallas_call(

time: 65.8 us -> 64.6 us (0.982)
  Pallas kernels: 65 us -> 63.8 us
    pallas_call x1, Pallas kernels: 63.6 us -> 62.5 us  [local(): pl.pallas_call(kernel, out_shape=(out, out, out), in_specs=[pl.BlockSpec(...]
where the time goes in v4:
time: 64.6 us; the launch traced here: 64.5 us
  Pallas kernels  63.8 us (99%)
    pallas_call x1, Pallas kernels, local(): pl.pallas_call(kernel, out_shape=(out, out, out), in_specs=[pl.BlockSpec(...  62.5 us
    pallas_call x1, Pallas kernels, local(): pl.pallas_call(hand_out, out_shape=(out, out, out), in_specs=[vmem] * 3,...  1.34 us

profile of v4, /device:TPU:1, one launch (start us, length us, event | category | flops | bytes accessed | tf_op | source)
XLA Modules:
  0.0 64.5 jit_solution(7109856359450153380)
XLA Ops:
  0.6 62.5 %shard_map.94 = (f32[16,128]{1,0:T(8,128)}, f32[16,128]{1,0:T(8,128)}, f32[16,128]{1,0:T(8,128)}) custom-call(f32[16,128]{1,0:T(8,128)} %points_hbm.1, f32[16]{0:T(128)} %ls_hbm.1, f32[2]{0:T(128)} %var_hbm.1, f32[128,128]{1,0:T(8,128)} %factor_hbm.1, f32[16,128]{1,0:T(8,128)} %solution_hbm.1, f32[16,128]{1,0:T(8,128)} %residual_hbm.1, f32[16,128]{1,0:T(8,128)} %direction_hbm.1), custom_call_target="tpu_custom_call" | custom-call | tf_op jit(solution)/shard_map/pallas_call | solution.py:607
  63.1 1.3 %shard_map.95 = (f32[16,128]{1,0:T(8,128)}, f32[16,128]{1,0:T(8,128)}, f32[16,128]{1,0:T(8,128)}) custom-call(f32[16,128]{1,0:T(8,128)} %get-tuple-element.6.refs_0_, f32[16,128]{1,0:T(8,128)} %get-tuple-element.7.refs_1_, f32[16,128]{1,0:T(8,128)} %get-tuple-element.8.refs_2_), custom_call_target="tpu_custom_call" | custom-call | tf_op jit(solution)/shard_map/pallas_call | solution.py:619

commit v5 on v4

--- a/solution.py
+++ b/solution.py
@@ -72,7 +72,7 @@
     t_a, t_b, h_a, h_b, l_a, l_b, ft_a, ft_b, fh_a, fh_b, fl_a, fl_b,
     left, right, right_f, lsend, lrx, rsend, rrx, hub_rx, hub_out, hub_in,
     g_send, g_rx, g_piece, g_zx, g_window, g_zy, g_tot, g_all, core_ref,
-    v_give, v_take, v_chip, v_px, v_plane, v_zx, v_window, v_zy, v_all,
+    v_half, v_px, v_plane, v_zx, v_window, v_zy, v_all,
     in_sem, send_sem, recv_sem, item_sem,
 ):
     nz, npl = Z_HI * Z_LO, X * Y * 2
@@ -495,25 +495,16 @@
     for n, (a, b) in enumerate(products):
         scalars = jnp.where(lane16 == rem(sub16, 8) * 4 + n, jnp.sum(a * b, axis=1, keepdims=True), scalars)
 
-    def half_of(c):
-        first = c == 0
-        rows = jnp.where(first, proj_im[0:8], proj_im[8:16])
-        inner = jnp.where(first, scalars[0:8], scalars[8:16])
-        return rows, jnp.sum(inner, axis=0, keepdims=True)
-
-    for ref, (rows, inner) in ((v_give, half_of(1 - core)), (v_chip, half_of(core))):
+    for c in range(2):
         for p in range(8):
-            ref[p] = rows[p : p + 1]
-        ref[8] = inner
-    send(7, v_give, v_take, other_core())
-    wait(recv_sem, 7, v_take)
-    v_chip[...] += v_take[...]
-    loop(1, half_np, lambda m: send(8, v_chip, v_px.at[m], in_plane(2 * m)))
+            v_half[c, p] = proj_im[8 * c + p : 8 * c + p + 1]
+        v_half[c, 8] = jnp.sum(scalars[8 * c : 8 * c + 8], axis=0, keepdims=True)
+    loop(1, npl, lambda j: send(8, v_half.at[rem(s + j, 2)], v_px.at[j], in_plane(j)))
     loop(16, 60, sweep)
-    wait(recv_sem, 8, v_px.at[pl.ds(1, half_np - 1)])
-    total = v_chip[...]
-    for m in range(1, half_np):
-        total = total + v_px[m]
+    wait(recv_sem, 8, v_px.at[pl.ds(1, npl - 1)])
+    total = v_half[core]
+    for j in range(1, npl):
+        total = total + v_px[j]
     v_plane[...] = total
     window(9, v_plane, v_zx)
     loop(60, 96, sweep)
@@ -563,8 +554,7 @@
     wait(send_sem, 4, g_zx)
     wait(send_sem, 5, g_rx.at[pl.ds(1, npl - 1)])
     wait(send_sem, 6, lrx.at[pl.ds(1, npl - 1)])
-    wait(send_sem, 7, v_take)
-    wait(send_sem, 8, v_px.at[pl.ds(1, half_np - 1)])
+    wait(send_sem, 8, v_px.at[pl.ds(1, npl - 1)])
     wait(send_sem, 9, v_zx)
     wait(send_sem, 11, hub_rx)
     wait(send_sem, 12, hub_in)
@@ -600,7 +590,7 @@
         ((npl, gr, 128), F32), ((npl, gr, 128), F32), ((gr, 128), F32), ((blocks - 1, gr, 128), F32),
         ((gr, 128), F32), ((2, gr, 128), F32),
         ((gr, 128), F32), ((npl, gr, 128), F32), ((128, 128), F32),
-        (vr, F32), (vr, F32), (vr, F32), ((npl // 2, *vr), F32), (vr, F32), ((blocks - 1, *vr), F32), (vr, F32),
+        ((2, *vr), F32), ((npl, *vr), F32), (vr, F32), ((blocks - 1, *vr), F32), (vr, F32),
         ((2, 2, *vr), F32), ((2, *vr), F32),
     ]
     out = jax.ShapeDtypeStruct(direction.shape, F32)

time: 64.6 us -> 64.4 us (level)
  no operation moved by 1% of the time
where the time goes in v5:
time: 64.4 us; the launch traced here: 64.2 us
  Pallas kernels  63.6 us (99%)
    pallas_call x1, Pallas kernels, local(): pl.pallas_call(kernel, out_shape=(out, out, out), in_specs=[pl.BlockSpec(...  62.3 us
    pallas_call x1, Pallas kernels, local(): pl.pallas_call(hand_out, out_shape=(out, out, out), in_specs=[vmem] * 3,...  1.34 us

profile of v5, /device:TPU:1, one launch (start us, length us, event | category | flops | bytes accessed | tf_op | source)
XLA Modules:
  0.0 64.2 jit_solution(6164690568368273483)
XLA Ops:
  0.6 62.3 %shard_map.94 = (f32[16,128]{1,0:T(8,128)}, f32[16,128]{1,0:T(8,128)}, f32[16,128]{1,0:T(8,128)}) custom-call(f32[16,128]{1,0:T(8,128)} %points_hbm.1, f32[16]{0:T(128)} %ls_hbm.1, f32[2]{0:T(128)} %var_hbm.1, f32[128,128]{1,0:T(8,128)} %factor_hbm.1, f32[16,128]{1,0:T(8,128)} %solution_hbm.1, f32[16,128]{1,0:T(8,128)} %residual_hbm.1, f32[16,128]{1,0:T(8,128)} %direction_hbm.1), custom_call_target="tpu_custom_call" | custom-call | tf_op jit(solution)/shard_map/pallas_call | solution.py:597
  62.9 1.3 %shard_map.95 = (f32[16,128]{1,0:T(8,128)}, f32[16,128]{1,0:T(8,128)}, f32[16,128]{1,0:T(8,128)}) custom-call(f32[16,128]{1,0:T(8,128)} %get-tuple-element.6.refs_0_, f32[16,128]{1,0:T(8,128)} %get-tuple-element.7.refs_1_, f32[16,128]{1,0:T(8,128)} %get-tuple-element.8.refs_2_), custom_call_target="tpu_custom_call" | custom-call | tf_op jit(solution)/shard_map/pallas_call | solution.py:609
